TPU v7x, 256 devices: a whole 4x4x8 slice. The times are simulated.
256 devices in a mesh: wide: 32 (over z, x_hi, core), narrow: 8 (over x_lo, y).
Axes of the slice: x: 4 (x_hi: 2, x_lo: 2; x = x_hi * 2 + x_lo), y: 4, z: 8, core: 2. Of those that a mesh axis runs over, the one named last changes fastest.
Arguments:
- patches: bfloat16 [1024, 256, 1152], P('wide'), may hold values from -6 to 6
- w_key: bfloat16 [1152, 1152], P(None, 'narrow'), may hold values from -0.1875 to 0.1875
- w_value: bfloat16 [1152, 1152], P(None, 'narrow'), may hold values from -0.1875 to 0.1875
- w_out: bfloat16 [1152, 1152], P('narrow'), may hold values from -0.1875 to 0.1875
- probe: bfloat16 [1152], P('narrow'), may hold values from -64 to 64
- texts: bfloat16 [1024, 1152], P(('wide', 'narrow')), may hold values from -6 to 6
Outputs:
- row_loss: float32 [1024], P(('wide', 'narrow'))
- text_grad: float32 [1024, 1152], P(('wide', 'narrow'))
- grad_key: float32 [1152, 1152], P('wide', 'narrow')
- grad_value: float32 [1152, 1152], P('wide', 'narrow')
- grad_out: float32 [1152, 1152], P('narrow', 'wide')
All inputs are finite; a program needn't handle non-finite values.
Results may differ from a plain program's by a relative error of at most 0.027.
The roundings to bfloat16 on the way count: a program that leaves them out, or rounds other values in their place, can miss the bound.
Values may be sent and summed in bfloat16 or wider, within the bound.
A program may use at most 128 MiB of HBM per device.

v0:
```python
import math

import jax
import jax.numpy as jnp
from jax import lax
from jax.sharding import PartitionSpec as P

D = 1152
HEAD_DIM = 72
PATCHES = 256


logit_scale = 16.0
logit_bias = -4.0


def shortened(shard):

    def short(part):
        return part.astype(jnp.bfloat16) if part.dtype == jnp.float32 else part

    return jax.tree.map(short, shard)


def passed_along(block, axis, distance):
    devices = range(lax.axis_size(axis))
    route = [((i - distance) % len(devices), i) for i in devices]
    return lax.ppermute(block, axis, route)


def pair_coef(image_low, text_block, image_ids, text_ids):
    logits = (
        logit_scale * jnp.dot(image_low, text_block.T, preferred_element_type=jnp.float32)
        + logit_bias
    )
    signs = jnp.where(image_ids[:, None] == text_ids[None, :], 1.0, -1.0).astype(jnp.float32)
    loss_part = jnp.sum(jax.nn.softplus(-signs * logits), axis=1)
    coef = -signs * jax.nn.sigmoid(-signs * logits)
    return (loss_part, coef)


def pair_terms(image_low, text_block, image_ids, text_ids):
    loss_part, coef = pair_coef(image_low, text_block, image_ids, text_ids)
    image_part = logit_scale * jnp.dot(
        coef, text_block.astype(jnp.float32), precision=lax.Precision.HIGHEST
    )
    text_part = logit_scale * jnp.dot(
        coef.T, image_low.astype(jnp.float32), precision=lax.Precision.HIGHEST
    )
    return (loss_part, image_part, text_part)


def shards(patches, w_key, w_value, w_out, probe, texts):
    n_wide = lax.axis_size("wide")
    n_narrow = lax.axis_size("narrow")
    my_wide = lax.axis_index("wide")
    my_narrow = lax.axis_index("narrow")
    group = patches.shape[0]
    rows_own = texts.shape[0]
    local_width = w_key.shape[1]
    local_heads = local_width // HEAD_DIM
    root_scale = 1.0 / math.sqrt(HEAD_DIM)
    w_both = jnp.concatenate([w_key, w_value], axis=1)
    probe_heads = probe.reshape(local_heads, HEAD_DIM)
    flat_rows = patches.reshape(group * PATCHES, D)
    both_rows = jnp.dot(flat_rows, w_both, preferred_element_type=jnp.float32).astype(jnp.bfloat16)
    key_rows = both_rows[:, :local_width].reshape(group, PATCHES, local_heads, HEAD_DIM)
    value_rows = both_rows[:, local_width:].reshape(group, PATCHES, local_heads, HEAD_DIM)
    scores = (
        jnp.einsum("gphc,hc->ghp", key_rows, probe_heads, preferred_element_type=jnp.float32)
        * root_scale
    )
    weights = jax.nn.softmax(scores, axis=-1)
    weights_low = weights.astype(jnp.bfloat16)
    heads_out = jnp.einsum(
        "ghp,gphc->ghc", weights_low, value_rows, preferred_element_type=jnp.float32
    )
    heads_out = heads_out.astype(jnp.bfloat16).reshape(group, local_width)
    partial_out = jnp.dot(heads_out, w_out, preferred_element_type=jnp.float32)
    pooled = lax.psum_scatter(partial_out, "narrow", scatter_dimension=0, tiled=True)
    pooled_norm = jnp.sqrt(jnp.sum(pooled * pooled, axis=1, keepdims=True) + 1e-06)
    image_unit = pooled / pooled_norm
    image_low = image_unit.astype(jnp.bfloat16)
    text_float = texts.astype(jnp.float32)
    text_norm = jnp.sqrt(jnp.sum(text_float * text_float, axis=1, keepdims=True) + 1e-06)
    text_unit = text_float / text_norm
    text_low = text_unit.astype(jnp.bfloat16)
    image_ids = my_wide * group + my_narrow * rows_own + jnp.arange(rows_own, dtype=jnp.int32)
    text_group = lax.all_gather(text_low, "wide", axis=0, tiled=True)
    span = n_wide * rows_own
    offsets = jnp.arange(span, dtype=jnp.int32)
    wide_part = offsets // rows_own * group + offsets % rows_own
    row_loss = jnp.zeros((rows_own,), jnp.float32)
    image_grad = jnp.zeros((rows_own, D), jnp.float32)
    carried = jnp.zeros((span, D), jnp.float32)
    text_block = text_group
    for rotation in range(n_narrow):
        anchor = (my_narrow - rotation) % n_narrow
        text_ids = wide_part + anchor * rows_own
        loss_part, image_part, text_part = pair_terms(image_low, text_block, image_ids, text_ids)
        row_loss = row_loss + loss_part
        image_grad = image_grad + image_part
        carried = passed_along(shortened(carried + text_part), "narrow", 1)
        if rotation + 1 < n_narrow:
            text_block = passed_along(text_block, "narrow", 1)
    unit_grad = lax.psum_scatter(
        carried.astype(jnp.bfloat16), "wide", scatter_dimension=0, tiled=True
    ).astype(jnp.float32)
    text_grad = (
        unit_grad - text_unit * jnp.sum(text_unit * unit_grad, axis=1, keepdims=True)
    ) / text_norm
    pooled_grad = (
        (image_grad - image_unit * jnp.sum(image_unit * image_grad, axis=1, keepdims=True))
        / pooled_norm
    ).astype(jnp.bfloat16)
    group_grad = lax.all_gather(pooled_grad, "narrow", axis=0, tiled=True)
    head_grad = jnp.dot(group_grad, w_out.T, preferred_element_type=jnp.float32).reshape(
        group, local_heads, HEAD_DIM
    )
    out_term = jnp.dot(heads_out.T, group_grad, preferred_element_type=jnp.float32)
    value_grad = jnp.einsum("ghp,ghc->gphc", weights_low.astype(jnp.float32), head_grad).astype(
        jnp.bfloat16
    )
    weight_grad = jnp.einsum(
        "ghc,gphc->ghp", head_grad, value_rows, precision=lax.Precision.HIGHEST
    )
    score_grad = weights * (weight_grad - jnp.sum(weights * weight_grad, axis=-1, keepdims=True))
    key_grad = (
        jnp.einsum("ghp,hc->gphc", score_grad, probe_heads.astype(jnp.float32)) * root_scale
    ).astype(jnp.bfloat16)
    both_grad = jnp.concatenate(
        [
            key_grad.reshape(group * PATCHES, local_width),
            value_grad.reshape(group * PATCHES, local_width),
        ],
        axis=1,
    )
    summed = lax.psum_scatter(
        lax.dot_general(
            flat_rows, both_grad, (((0,), (0,)), ((), ())), preferred_element_type=jnp.float32
        ),
        "wide",
        scatter_dimension=0,
        tiled=True,
    )
    grad_out = lax.psum_scatter(
        out_term.astype(jnp.bfloat16), "wide", scatter_dimension=1, tiled=True
    ).astype(jnp.float32)
    return (row_loss, text_grad, summed[:, :local_width], summed[:, local_width:], grad_out)


def solution(mesh):
    return jax.shard_map(
        shards,
        mesh=mesh,
        in_specs=(
            P("wide", None, None),
            P(None, "narrow"),
            P(None, "narrow"),
            P("narrow", None),
            P("narrow"),
            P(("wide", "narrow"), None),
        ),
        out_specs=(
            P(("wide", "narrow")),
            P(("wide", "narrow"), None),
            P("wide", "narrow"),
            P("wide", "narrow"),
            P("narrow", "wide"),
        ),
        check_vma=False,
    )
```

profile of v0, /device:TPU:1, one launch (start us, length us, event | category | flops | bytes accessed | tf_op | source)
XLA Modules:
  0.0 762.3 jit_solution(12900771834862998571)
XLA Ops:
  7.2 10.3 %fusion.4 = bf16[8192,288]{0,1:T(8,128)(2,1)S(1)} fusion(bf16[8192,1152]{1,0:T(8,128)(2,1)} %bitcast.120, bf16[1152,144]{0,1:T(8,128)(2,1)} %param.8, bf16[1152,144]{0,1:T(8,128)(2,1)} %param.7), kind=kOutput, calls=%fused_computation.4 | convolution fusion | flops 5439504384 | bytes 24256512 | tf_op jit(solution)/shard_map/dot_general | solution.py:66
  17.6 1.8 fusion.75
  19.4 0.7 copy.32
  20.1 2.3 copy.31
  22.5 1.4 fusion.13
  24.1 2.6 fusion.18
  26.8 0.8 fusion.78
  27.9 47.0 %all-gather = bf16[32,4,1152]{2,1,0:T(4,128)(2,1)S(1)} all-gather(bf16[1,4,1152]{2,1,0:T(4,128)(2,1)S(1)} %convert_bitcast_fusion.1), channel_id=1, replica_groups=mesh['wide'=32,'narrow'=8] {'wide'}, dimensions={0}, use_global_device_ids=true | all-gather | bytes 304128 | tf_op jit(solution)/shard_map/all_gather | solution.py:89
  75.0 1.2 collective-permute-start
  76.4 0.6 dynamic-slice
  77.7 0.6 fusion.77
  80.2 23.2 %all-reduce.9.cloned.1.call-done = f32[32,1152]{1,0:T(8,128)} async-done(((f32[32,1152]{1,0:T(8,128)}), f32[32,1152]{1,0:T(8,128)}) %all-reduce.9.cloned.1.call-update) | async-done | bytes 147472
  103.5 0.9 multiply_reduce_fusion.1
  104.4 0.8 fusion.74
  105.6 0.5 fusion.12
  106.5 1.8 collective-permute-start.1
  108.3 1.3 fusion.58
  109.6 1.3 convolution_add_fusion.6
  110.9 3.0 collective-permute-done.7
  113.9 0.5 add_convert_fusion.6
  114.5 3.0 collective-permute-done.1
  118.2 0.5 convolution_multiply_fusion.5
  118.7 7.0 collective-permute-done.8
  125.9 6.2 collective-permute-done.2
  132.7 0.5 convolution_multiply_fusion.4
  133.2 5.1 collective-permute-done.9
  138.5 6.2 collective-permute-done.3
  145.3 0.5 convolution_multiply_fusion.3
  145.9 5.1 collective-permute-done.10
  151.1 6.2 collective-permute-done.4
  158.0 0.5 convolution_multiply_fusion.2
  158.5 5.1 collective-permute-done.11
  163.8 6.2 collective-permute-done.5
  170.6 0.5 convolution_multiply_fusion.1
  171.2 5.1 collective-permute-done.12
  176.3 0.8 add_convert_fusion.1
  177.2 5.4 collective-permute-done.6
  182.9 0.4 multiply_reduce_fusion
  183.4 22.8 %all-gather.1 = bf16[8,4,1152]{2,1,0:T(4,128)(2,1)S(1)} all-gather(bf16[1,4,1152]{2,1,0:T(4,128)(2,1)S(1)} %fusion.54), channel_id=1, replica_groups=mesh['wide'=32,'narrow'=8] {'narrow'}, dimensions={0}, use_global_device_ids=true | all-gather | bytes 82944 | tf_op jit(solution)/shard_map/all_gather | solution.py:116
  206.6 4.0 fusion.16
  210.6 0.5 convolution_multiply_fusion
  211.2 0.8 multiply_convert_fusion
  212.0 1.0 add_convert_fusion
  213.4 3.0 copy.34
  216.4 0.5 multiply_convert_fusion.1
  216.9 3.0 copy.33
  219.9 1.0 collective-permute-done.14
  220.9 0.7 copy-done.1
  221.9 15.1 %fusion.9 = f32[1152,288]{0,1:T(8,128)} fusion(bf16[8192,1152]{1,0:T(8,128)(2,1)} %bitcast.121, bf16[8192,144]{0,1:T(8,128)(2,1)} %bitcast.114, bf16[8192,144]{0,1:T(8,128)(2,1)} %bitcast.115), kind=kOutput, calls=%fused_computation.11 | convolution fusion | flops 5445255168 | bytes 24920064 | tf_op jit(solution)/shard_map/dot_general | solution.py:139
  237.5 82.5 %fusion = bf16[144,40]{0,1:T(8,128)(2,1)S(1)} fusion(bf16[144,1152]{0,1:T(8,128)(2,1)S(1)} %convolution_convert_fusion.1), kind=kCustom, calls=%all-reduce-scatter | all-reduce-scatter fusion | flops 184321 | bytes 344320
  319.9 1.3 collective-permute-start.17
  321.2 1.3 collective-permute-start.16
  322.5 5.3 collective-permute-start.15
  327.9 1.3 collective-permute-start.18
  329.2 0.5 add_add_fusion
  330.2 0.5 concatenate.8
  330.8 0.6 dynamic-slice_convert_fusion
  331.4 153.6 %all-reduce.11.cloned.1.call-done = bf16[128,1152]{1,0:T(8,128)(2,1)} async-done(((bf16[128,1152]{1,0:T(8,128)(2,1)}), bf16[128,1152]{1,0:T(8,128)(2,1)}) %all-reduce.11.cloned.1.call-update) | async-done | bytes 294928
  485.0 0.9 fusion.51
  485.9 1.4 fusion.52
  487.3 265.5 %all-reduce.13.cloned.1.call-done = f32[1152,288]{0,1:T(8,128)} async-done(((f32[1152,288]{0,1:T(8,128)}), f32[1152,288]{0,1:T(8,128)}) %all-reduce.13.cloned.1.call-update) | async-done | bytes 1327120
  752.8 1.1 fusion.76
  753.9 0.7 copy.18
  754.6 0.7 copy.19
  (82 shorter events, 8.1 us)
Async XLA Ops:
  7.2 19.6 %copy-start = (bf16[144,1152]{1,0:T(8,128)(2,1)S(1)}, bf16[144,1152]{1,0:T(8,128)(2,1)}, u32[]{:S(2)}) copy-start(bf16[144,1152]{1,0:T(8,128)(2,1)} %param.9) | copy-start | bytes 995332
  7.2 96.3 %all-reduce.9.cloned.1.call-start = ((), (), s32[]{:S(2)}) async-start(), calls=%async_computation | async-start | bytes 294912
  19.4 0.7 copy-start.4
  23.9 3.9 copy-start.2
  24.0 52.4 %copy-start.5 = (u32[256]{0:T(256)S(1)}, u32[256]{0:T(256)}, u32[]{:S(2)}) copy-start(u32[256]{0:T(256)} %constant.149) | copy-start | bytes 3076
  24.1 53.6 %copy-start.3 = (u32[256]{0:T(256)S(1)}, u32[256]{0:T(256)}, u32[]{:S(2)}) copy-start(u32[256]{0:T(256)} %constant.153) | copy-start | bytes 3076
  27.7 457.3 %all-reduce.11.cloned.1.call-start = ((), (), s32[]{:S(2)}) async-start(), calls=%async_computation.1 | async-start | bytes 589824
  75.0 31.5 %collective-permute-start = (bf16[128,1152]{1,0:T(8,128)(2,1)S(1)}, bf16[128,1152]{1,0:T(8,128)(2,1)}, u32[]{:S(2)}, u32[]{:S(2)}) collective-permute-start(bf16[128,1152]{1,0:T(8,128)(2,1)S(1)} %reshape.108), channel_id=1, source_target_pairs={{7,0},{0,1},{1,2},{2,3},{3,4},{4,5},{5,6},{6,7},{15,8},{8,9},{9,10... | collective-permute-start | bytes 884744 | tf_op jit(solution)/shard_map/ppermute | solution.py:28
  106.1 7.8 %collective-permute-start.7 = (bf16[128,1152]{1,0:T(8,128)(2,1)S(1)}, bf16[128,1152]{1,0:T(8,128)(2,1)S(1)}, u32[]{:S(2)}, u32[]{:S(2)}) collective-permute-start(bf16[128,1152]{1,0:T(8,128)(2,1)S(1)} %fusion.12), channel_id=1, source_target_pairs={{7,0},{0,1},{1,2},{2,3},{3,4},{4,5},{5,6},{6,7},{15,8},{8,9},{9,10... | collective-permute-start | bytes 884744 | tf_op jit(solution)/shard_map/ppermute | solution.py:28
  106.5 11.0 %collective-permute-start.1 = (bf16[128,1152]{1,0:T(8,128)(2,1)}, bf16[128,1152]{1,0:T(8,128)(2,1)S(1)}, u32[]{:S(2)}, u32[]{:S(2)}) collective-permute-start(bf16[128,1152]{1,0:T(8,128)(2,1)} %collective-permute-done), channel_id=1, source_target_pairs={{7,0},{0,1},{1,2},{2,3},{3,4},{4,5},{5,6},{6,7},{15,8},{8,9},{9,10... | collective-permute-start | bytes 884744 | tf_op jit(solution)/shard_map/ppermute | solution.py:28
  114.4 11.3 %collective-permute-start.8 = (bf16[128,1152]{1,0:T(8,128)(2,1)S(1)}, bf16[128,1152]{1,0:T(8,128)(2,1)S(1)}, u32[]{:S(2)}, u32[]{:S(2)}) collective-permute-start(bf16[128,1152]{1,0:T(8,128)(2,1)S(1)} %add_convert_fusion.6), channel_id=1, source_target_pairs={{7,0},{0,1},{1,2},{2,3},{3,4},{4,5},{5,6},{6,7},{15,8},{8,9},{9,10... | collective-permute-start | bytes 884744 | tf_op jit(solution)/shard_map/ppermute | solution.py:28
  117.5 14.5 %collective-permute-start.2 = (bf16[128,1152]{1,0:T(8,128)(2,1)S(1)}, bf16[128,1152]{1,0:T(8,128)(2,1)S(1)}, u32[]{:S(2)}, u32[]{:S(2)}) collective-permute-start(bf16[128,1152]{1,0:T(8,128)(2,1)S(1)} %collective-permute-done.1), channel_id=1, source_target_pairs={{7,0},{0,1},{1,2},{2,3},{3,4},{4,5},{5,6},{6,7},{15,8},{8,9},{9,10... | collective-permute-start | bytes 884744 | tf_op jit(solution)/shard_map/ppermute | solution.py:28
  125.8 12.6 %collective-permute-start.9 = (bf16[128,1152]{1,0:T(8,128)(2,1)S(1)}, bf16[128,1152]{1,0:T(8,128)(2,1)S(1)}, u32[]{:S(2)}, u32[]{:S(2)}) collective-permute-start(bf16[128,1152]{1,0:T(8,128)(2,1)S(1)} %add_convert_fusion.5), channel_id=1, source_target_pairs={{7,0},{0,1},{1,2},{2,3},{3,4},{4,5},{5,6},{6,7},{15,8},{8,9},{9,10... | collective-permute-start | bytes 884744 | tf_op jit(solution)/shard_map/ppermute | solution.py:28
  132.0 12.6 %collective-permute-start.3 = (bf16[128,1152]{1,0:T(8,128)(2,1)S(1)}, bf16[128,1152]{1,0:T(8,128)(2,1)S(1)}, u32[]{:S(2)}, u32[]{:S(2)}) collective-permute-start(bf16[128,1152]{1,0:T(8,128)(2,1)S(1)} %collective-permute-done.2), channel_id=1, source_target_pairs={{7,0},{0,1},{1,2},{2,3},{3,4},{4,5},{5,6},{6,7},{15,8},{8,9},{9,10... | collective-permute-start | bytes 884744 | tf_op jit(solution)/shard_map/ppermute | solution.py:28
  138.4 12.6 %collective-permute-start.10 = (bf16[128,1152]{1,0:T(8,128)(2,1)S(1)}, bf16[128,1152]{1,0:T(8,128)(2,1)S(1)}, u32[]{:S(2)}, u32[]{:S(2)}) collective-permute-start(bf16[128,1152]{1,0:T(8,128)(2,1)S(1)} %add_convert_fusion.4), channel_id=1, source_target_pairs={{7,0},{0,1},{1,2},{2,3},{3,4},{4,5},{5,6},{6,7},{15,8},{8,9},{9,10... | collective-permute-start | bytes 884744 | tf_op jit(solution)/shard_map/ppermute | solution.py:28
  144.7 12.6 %collective-permute-start.4 = (bf16[128,1152]{1,0:T(8,128)(2,1)S(1)}, bf16[128,1152]{1,0:T(8,128)(2,1)S(1)}, u32[]{:S(2)}, u32[]{:S(2)}) collective-permute-start(bf16[128,1152]{1,0:T(8,128)(2,1)S(1)} %collective-permute-done.3), channel_id=1, source_target_pairs={{7,0},{0,1},{1,2},{2,3},{3,4},{4,5},{5,6},{6,7},{15,8},{8,9},{9,10... | collective-permute-start | bytes 884744 | tf_op jit(solution)/shard_map/ppermute | solution.py:28
  151.0 12.6 %collective-permute-start.11 = (bf16[128,1152]{1,0:T(8,128)(2,1)S(1)}, bf16[128,1152]{1,0:T(8,128)(2,1)S(1)}, u32[]{:S(2)}, u32[]{:S(2)}) collective-permute-start(bf16[128,1152]{1,0:T(8,128)(2,1)S(1)} %add_convert_fusion.3), channel_id=1, source_target_pairs={{7,0},{0,1},{1,2},{2,3},{3,4},{4,5},{5,6},{6,7},{15,8},{8,9},{9,10... | collective-permute-start | bytes 884744 | tf_op jit(solution)/shard_map/ppermute | solution.py:28
  157.3 12.6 %collective-permute-start.5 = (bf16[128,1152]{1,0:T(8,128)(2,1)S(1)}, bf16[128,1152]{1,0:T(8,128)(2,1)S(1)}, u32[]{:S(2)}, u32[]{:S(2)}) collective-permute-start(bf16[128,1152]{1,0:T(8,128)(2,1)S(1)} %collective-permute-done.4), channel_id=1, source_target_pairs={{7,0},{0,1},{1,2},{2,3},{3,4},{4,5},{5,6},{6,7},{15,8},{8,9},{9,10... | collective-permute-start | bytes 884744 | tf_op jit(solution)/shard_map/ppermute | solution.py:28
  163.7 12.6 %collective-permute-start.12 = (bf16[128,1152]{1,0:T(8,128)(2,1)S(1)}, bf16[128,1152]{1,0:T(8,128)(2,1)S(1)}, u32[]{:S(2)}, u32[]{:S(2)}) collective-permute-start(bf16[128,1152]{1,0:T(8,128)(2,1)S(1)} %add_convert_fusion.2), channel_id=1, source_target_pairs={{7,0},{0,1},{1,2},{2,3},{3,4},{4,5},{5,6},{6,7},{15,8},{8,9},{9,10... | collective-permute-start | bytes 884744 | tf_op jit(solution)/shard_map/ppermute | solution.py:28
  170.0 12.6 %collective-permute-start.6 = (bf16[128,1152]{1,0:T(8,128)(2,1)S(1)}, bf16[128,1152]{1,0:T(8,128)(2,1)S(1)}, u32[]{:S(2)}, u32[]{:S(2)}) collective-permute-start(bf16[128,1152]{1,0:T(8,128)(2,1)S(1)} %collective-permute-done.5), channel_id=1, source_target_pairs={{7,0},{0,1},{1,2},{2,3},{3,4},{4,5},{5,6},{6,7},{15,8},{8,9},{9,10... | collective-permute-start | bytes 884744 | tf_op jit(solution)/shard_map/ppermute | solution.py:28
  177.0 35.0 %collective-permute-start.13 = (bf16[128,1152]{1,0:T(8,128)(2,1)}, bf16[128,1152]{1,0:T(8,128)(2,1)}, u32[]{:S(2)}, u32[]{:S(2)}) collective-permute-start(bf16[128,1152]{1,0:T(8,128)(2,1)} %add_convert_fusion.1), channel_id=1, source_target_pairs={{7,0},{0,1},{1,2},{2,3},{3,4},{4,5},{5,6},{6,7},{15,8},{8,9},{9,10... | collective-permute-start | bytes 884744 | tf_op jit(solution)/shard_map/ppermute | solution.py:28
  213.1 7.8 %collective-permute-start.14 = (bf16[128,1152]{1,0:T(8,128)(2,1)S(1)}, bf16[128,1152]{1,0:T(8,128)(2,1)S(1)}, u32[]{:S(2)}, u32[]{:S(2)}) collective-permute-start(bf16[128,1152]{1,0:T(8,128)(2,1)S(1)} %add_convert_fusion), channel_id=1, source_target_pairs={{7,0},{0,1},{1,2},{2,3},{3,4},{4,5},{5,6},{6,7},{15,8},{8,9},{9,10... | collective-permute-start | bytes 884744 | tf_op jit(solution)/shard_map/ppermute | solution.py:28
  220.9 0.7 copy-start.1
  221.6 531.2 %all-reduce.13.cloned.1.call-start = ((), (), s32[]{:S(2)}) async-start(), calls=%async_computation.2 | async-start | bytes 2654208
  319.9 10.0 %collective-permute-start.17 = (bf16[144,40]{0,1:T(8,128)(2,1)S(1)}, bf16[144,40]{0,1:T(8,128)(2,1)S(1)}, u32[]{:S(2)}, u32[]{:S(2)}) collective-permute-start(bf16[144,40]{0,1:T(8,128)(2,1)S(1)} %fusion), channel_id=1, source_target_pairs={{0,24},{8,32},{16,40},{24,48},{32,56},{40,64},{48,72},{56,80},{64,... | collective-permute-start | bytes 34568
  321.2 8.7 %collective-permute-start.16 = (bf16[144,40]{0,1:T(8,128)(2,1)S(1)}, bf16[144,40]{0,1:T(8,128)(2,1)S(1)}, u32[]{:S(2)}, u32[]{:S(2)}) collective-permute-start(bf16[144,40]{0,1:T(8,128)(2,1)S(1)} %fusion), channel_id=1, source_target_pairs={{0,16},{8,24},{16,32},{24,40},{32,48},{40,56},{48,64},{56,72},{64,... | collective-permute-start | bytes 34568
  322.5 7.7 %collective-permute-start.15 = (bf16[144,40]{0,1:T(8,128)(2,1)S(1)}, bf16[144,40]{0,1:T(8,128)(2,1)S(1)}, u32[]{:S(2)}, u32[]{:S(2)}) collective-permute-start(bf16[144,40]{0,1:T(8,128)(2,1)S(1)} %fusion), channel_id=1, source_target_pairs={{0,8},{8,16},{16,24},{24,32},{32,40},{40,48},{48,56},{56,64},{64,7... | collective-permute-start | bytes 34568
  327.9 2.0 collective-permute-start.18
Sparse Core Ops, SparseCore 0:
  27.8 75.6 all-reduce.8
  221.7 263.1 all-reduce.10
  487.6 265.1 all-reduce.12
where the time goes:
time: 771 us; the launch traced here: 762 us
  waiting for transfers between devices  507 us (66%)
  blocking collectives  152 us (20%)
  matrix products  46.4 us (6%)
  between operations  17.3 us (2%)
  local copies, waits for them, and re-layouts  16.5 us (2%)
  starting transfers between devices  13.3 us (2%)
  other arithmetic  9.21 us (1%)
    unnamed x10, waiting for transfers between devices  443 us
    unnamed x1, blocking collectives  82.5 us
    ppermute x15, waiting for transfers between devices, passed_along(): return lax.ppermute(block, axis, route)  64.5 us
    all_gather x1, blocking collectives, shards(): text_group = lax.all_gather(text_low, 'wide', axis=0, tiled=True)  47 us
    all_gather x1, blocking collectives, shards(): group_grad = lax.all_gather(pooled_grad, 'narrow', axis=0, tiled=True)  22.8 us
  transfers between devices with their start and end apart: 22, of which 18 were waited for; matrix products, arithmetic and copies ran while one was open for 17% of the time, Pallas kernels for 0%

commit v1 on v0

v1 whole, which is shorter than its diff:
```python
import functools
import math

import jax
import jax.numpy as jnp
from jax import lax
from jax.experimental import pallas as pl
from jax.experimental.pallas import tpu as pltpu
from jax.sharding import PartitionSpec as P

D = 1152
HEAD_DIM = 72
PATCHES = 256
QUAD = 4
ROWS = 4
MESH = pl.DeviceIdType.MESH

logit_scale = 16.0
logit_bias = -4.0


def remote(src, dst, send, recv, device):
    copy = pltpu.make_async_remote_copy(
        src_ref=src,
        dst_ref=dst,
        send_sem=send,
        recv_sem=recv,
        device_id=device,
        device_id_type=MESH,
    )
    copy.start()
    return copy


def split_dot(coef, other, dims):
    high = coef.astype(jnp.bfloat16)
    rest = coef - high.astype(jnp.float32)
    mid = rest.astype(jnp.bfloat16)
    low = (rest - mid.astype(jnp.float32)).astype(jnp.bfloat16)
    dot = lambda part: lax.dot_general(part, other, dims, preferred_element_type=jnp.float32)
    return dot(low) + dot(mid) + dot(high)


def meet(devices):
    barrier = pltpu.get_barrier_semaphore()
    for device in devices:
        pl.semaphore_signal(barrier, inc=1, device_id=device, device_id_type=MESH)
    pl.semaphore_wait(barrier, len(devices))


def loss_kernel(
    nz, nn, partial, texts, loss_out, text_out, grad_out,
    rbuf, qbuf, tbuf, ibuf, gsrc, gbuf, usrc, ubuf, vsrc, vbuf, pbuf, nsend, nrecv, zsend, zrecv, qsend, qrecv,
):
    w, n = lax.axis_index("wide"), lax.axis_index("narrow")
    z, q = w // QUAD, lax.rem(w, QUAD)
    narrow_peers = [lax.rem(n + d, nn) for d in range(1, nn)]
    z_peers = [lax.rem(z + d, nz) for d in range(1, nz)]
    q_peers = [lax.rem(q + d, QUAD) for d in range(1, QUAD)]
    at_n = lambda k: {"wide": w, "narrow": k}
    at_z = lambda k: {"wide": k * QUAD + q, "narrow": n}
    at_q = lambda k: {"wide": z * QUAD + k, "narrow": n}
    meet([at_n(k) for k in narrow_peers] + [at_z(k) for k in z_peers] + [at_q(k) for k in q_peers])
    sent = []

    def exchange(peers, place, me, src, dst, send, recv):
        copies = [remote(src(k), dst.at[me], send.at[k], recv.at[me], place(k)) for k in peers]
        sent.extend(copies)

    def arrived(peers, buf, send, recv):
        for k in peers:
            pltpu.make_async_copy(buf.at[k], buf.at[k], recv.at[k]).wait()

    exchange(narrow_peers, at_n, n, lambda k: partial.at[k], rbuf, nsend.at[0], nrecv.at[0])
    text_float = texts[...].astype(jnp.float32)
    text_norm = jnp.sqrt(jnp.sum(text_float * text_float, axis=1, keepdims=True) + 1e-06)
    text_unit = text_float / text_norm
    qbuf[q] = text_unit.astype(jnp.bfloat16).astype(jnp.float32)
    exchange(q_peers, at_q, q, lambda k: qbuf.at[q], qbuf, qsend.at[0], qrecv.at[0])
    arrived(q_peers, qbuf, qsend.at[0], qrecv.at[0])
    tbuf[z] = jnp.concatenate([qbuf[k] for k in range(QUAD)], axis=0).astype(jnp.bfloat16)
    exchange(z_peers, at_z, z, lambda k: tbuf.at[z], tbuf, zsend.at[0], zrecv.at[0])

    arrived(narrow_peers, rbuf, nsend.at[0], nrecv.at[0])
    pooled = partial[n]
    for k in narrow_peers:
        pooled = pooled + rbuf[k]
    pooled_norm = jnp.sqrt(jnp.sum(pooled * pooled, axis=1, keepdims=True) + 1e-06)
    image_unit = pooled / pooled_norm
    ibuf[n] = image_unit.astype(jnp.bfloat16).astype(jnp.float32)
    exchange(narrow_peers, at_n, n, lambda k: ibuf.at[n], ibuf, nsend.at[1], nrecv.at[1])
    arrived(z_peers, tbuf, zsend.at[0], zrecv.at[0])
    arrived(narrow_peers, ibuf, nsend.at[1], nrecv.at[1])

    group, span = nn * ROWS, nz * QUAD * ROWS
    image_low = jnp.concatenate([ibuf[k] for k in range(nn)], axis=0).astype(jnp.bfloat16)
    text_low = tbuf[...].reshape(span, D)
    logits = (
        logit_scale
        * lax.dot_general(image_low, text_low, (((1,), (1,)), ((), ())), preferred_element_type=jnp.float32)
        + logit_bias
    )
    image_ids = w * group + lax.broadcasted_iota(jnp.int32, (group, span), 0)
    offsets = lax.broadcasted_iota(jnp.int32, (group, span), 1)
    text_ids = offsets // ROWS * group + n * ROWS + offsets % ROWS
    signs = jnp.where(image_ids == text_ids, 1.0, -1.0).astype(jnp.float32)
    margin = -signs * logits
    small = jnp.exp(-jnp.abs(margin))
    loss_part = jnp.sum(jnp.maximum(margin, 0.0) + jnp.log1p(small), axis=1, keepdims=True)
    coef = -signs * jnp.where(margin >= 0.0, 1.0, small) / (1.0 + small)
    image_part = logit_scale * split_dot(coef, text_low, (((1,), (0,)), ((), ())))
    for k in range(nn):
        gsrc[k, :, :D] = image_part[k * ROWS : (k + 1) * ROWS]
        gsrc[k, :, D:] = jnp.broadcast_to(loss_part[k * ROWS : (k + 1) * ROWS], (ROWS, 128))
    exchange(narrow_peers, at_n, n, lambda k: gsrc.at[k], gbuf, nsend.at[2], nrecv.at[2])
    text_part = logit_scale * split_dot(coef.T, image_low, (((1,), (0,)), ((), ())))
    usrc[...] = text_part.astype(jnp.bfloat16).reshape(nz, QUAD * ROWS, D)
    exchange(z_peers, at_z, z, lambda k: usrc.at[k], ubuf, zsend.at[1], zrecv.at[1])

    arrived(narrow_peers, gbuf, nsend.at[2], nrecv.at[2])
    both = gsrc[n]
    for k in narrow_peers:
        both = both + gbuf[k]
    loss_out[...] = both[:, D:]
    image_grad = both[:, :D]
    pooled_grad = (
        image_grad - image_unit * jnp.sum(image_unit * image_grad, axis=1, keepdims=True)
    ) / pooled_norm
    pbuf[n] = pooled_grad.astype(jnp.bfloat16).astype(jnp.float32)
    exchange(narrow_peers, at_n, n, lambda k: pbuf.at[n], pbuf, nsend.at[3], nrecv.at[3])

    arrived(z_peers, ubuf, zsend.at[1], zrecv.at[1])
    quad_grad = usrc[z].astype(jnp.float32)
    for k in z_peers:
        quad_grad = quad_grad + ubuf[k].astype(jnp.float32)
    for k in range(QUAD):
        vsrc[k] = quad_grad[k * ROWS : (k + 1) * ROWS]
    exchange(q_peers, at_q, q, lambda k: vsrc.at[k], vbuf, qsend.at[1], qrecv.at[1])
    arrived(narrow_peers, pbuf, nsend.at[3], nrecv.at[3])
    grad_out[...] = jnp.concatenate([pbuf[k] for k in range(nn)], axis=0).astype(jnp.bfloat16)
    arrived(q_peers, vbuf, qsend.at[1], qrecv.at[1])
    unit_grad = vsrc[q]
    for k in q_peers:
        unit_grad = unit_grad + vbuf[k]
    text_out[...] = (
        unit_grad - text_unit * jnp.sum(text_unit * unit_grad, axis=1, keepdims=True)
    ) / text_norm
    for copy in sent:
        copy.wait_send()


def loss_call(nz, nn, partial, texts):
    vmem = pl.BlockSpec(memory_space=pltpu.VMEM)
    f32, bf16 = jnp.float32, jnp.bfloat16
    return pl.pallas_call(
        functools.partial(loss_kernel, nz, nn),
        out_shape=(
            jax.ShapeDtypeStruct((ROWS, 128), f32),
            jax.ShapeDtypeStruct((ROWS, D), f32),
            jax.ShapeDtypeStruct((nn * ROWS, D), bf16),
        ),
        in_specs=[vmem] * 2,
        out_specs=(vmem,) * 3,
        scratch_shapes=[
            pltpu.VMEM((nn, ROWS, D), f32),
            pltpu.VMEM((QUAD, ROWS, D), f32),
            pltpu.VMEM((nz, QUAD * ROWS, D), bf16),
            pltpu.VMEM((nn, ROWS, D), f32),
            pltpu.VMEM((nn, ROWS, D + 128), f32),
            pltpu.VMEM((nn, ROWS, D + 128), f32),
            pltpu.VMEM((nz, QUAD * ROWS, D), bf16),
            pltpu.VMEM((nz, QUAD * ROWS, D), bf16),
            pltpu.VMEM((QUAD, ROWS, D), f32),
            pltpu.VMEM((QUAD, ROWS, D), f32),
            pltpu.VMEM((nn, ROWS, D), f32),
            pltpu.SemaphoreType.DMA((4, nn)),
            pltpu.SemaphoreType.DMA((4, nn)),
            pltpu.SemaphoreType.DMA((2, nz)),
            pltpu.SemaphoreType.DMA((2, nz)),
            pltpu.SemaphoreType.DMA((2, QUAD)),
            pltpu.SemaphoreType.DMA((2, QUAD)),
        ],
        compiler_params=pltpu.CompilerParams(
            collective_id=0, has_side_effects=True, vmem_limit_bytes=32 * 1024 * 1024
        ),
    )(partial, texts)


def sum_kernel(nz, grads, out, abuf, hsrc, hbuf, ssrc, sbuf, asend, arecv, zsend, zrecv, qsend, qrecv):
    w, n = lax.axis_index("wide"), lax.axis_index("narrow")
    z, q = w // QUAD, lax.rem(w, QUAD)
    core = lax.rem(q, 2)
    z_peers = [lax.rem(z + d, nz) for d in range(1, nz)]
    q_peers = [lax.rem(q + d, QUAD) for d in range(1, QUAD)]
    at_z = lambda k: {"wide": k * QUAD + q, "narrow": n}
    at_q = lambda k: {"wide": z * QUAD + k, "narrow": n}
    sibling = at_q(q + 1 - 2 * core)
    meet([at_z(k) for k in z_peers] + [at_q(k) for k in q_peers])
    sent = []
    order = z_peers + [z]
    for k in order:
        sent.append(remote(grads.at[1 - core, k], abuf.at[k], asend.at[k], arecv.at[k], sibling))
    for i, k in enumerate(order):
        pltpu.make_async_copy(abuf.at[k], abuf.at[k], arecv.at[k]).wait()
        total = grads[core, k] + abuf[k]
        if i < nz - 1:
            hsrc[k] = total.astype(hsrc.dtype)
            sent.append(remote(hsrc.at[k], hbuf.at[z], zsend.at[k], zrecv.at[z], at_z(k)))
    for k in reversed(z_peers):
        pltpu.make_async_copy(hbuf.at[k], hbuf.at[k], zrecv.at[k]).wait()
        total = total + hbuf[k].astype(jnp.float32)
    rows = total.shape[0] // QUAD
    for k in range(QUAD):
        ssrc[k] = total[k * rows : (k + 1) * rows]
    for k in q_peers:
        sent.append(remote(ssrc.at[k], sbuf.at[q], qsend.at[k], qrecv.at[q], at_q(k)))
    sbuf[q] = ssrc[q]
    for k in q_peers:
        pltpu.make_async_copy(sbuf.at[k], sbuf.at[k], qrecv.at[k]).wait()
    width = total.shape[1]
    out[:, :width] = sbuf[0] + sbuf[2]
    out[:, width:] = sbuf[1] + sbuf[3]
    for copy in sent:
        copy.wait_send()


def sum_call(nz, grads):
    vmem = pl.BlockSpec(memory_space=pltpu.VMEM)
    f32, bf16 = jnp.float32, jnp.bfloat16
    _, _, rows, width = grads.shape
    return pl.pallas_call(
        functools.partial(sum_kernel, nz),
        out_shape=jax.ShapeDtypeStruct((rows // QUAD, 2 * width), f32),
        in_specs=[vmem],
        out_specs=vmem,
        scratch_shapes=[
            pltpu.VMEM((nz, rows, width), f32),
            pltpu.VMEM((nz, rows, width), f32),
            pltpu.VMEM((nz, rows, width), f32),
            pltpu.VMEM((QUAD, rows // QUAD, width), f32),
            pltpu.VMEM((QUAD, rows // QUAD, width), f32),
            pltpu.SemaphoreType.DMA((nz,)),
            pltpu.SemaphoreType.DMA((nz,)),
            pltpu.SemaphoreType.DMA((nz,)),
            pltpu.SemaphoreType.DMA((nz,)),
            pltpu.SemaphoreType.DMA((QUAD,)),
            pltpu.SemaphoreType.DMA((QUAD,)),
        ],
        compiler_params=pltpu.CompilerParams(
            collective_id=1, has_side_effects=True, vmem_limit_bytes=32 * 1024 * 1024
        ),
    )(grads)


def shards(patches, w_key, w_value, w_out, probe, texts):
    nz = lax.axis_size("wide") // QUAD
    nn = lax.axis_size("narrow")
    group = patches.shape[0]
    local_width = w_key.shape[1]
    local_heads = local_width // HEAD_DIM
    root_scale = 1.0 / math.sqrt(HEAD_DIM)
    w_both = jnp.concatenate([w_key, w_value], axis=1)
    probe_heads = probe.reshape(local_heads, HEAD_DIM)
    flat_rows = patches.reshape(group * PATCHES, D)
    both_rows = jnp.dot(flat_rows, w_both, preferred_element_type=jnp.float32).astype(jnp.bfloat16)
    key_rows = both_rows[:, :local_width].reshape(group, PATCHES, local_heads, HEAD_DIM)
    value_rows = both_rows[:, local_width:].reshape(group, PATCHES, local_heads, HEAD_DIM)
    scores = (
        jnp.einsum("gphc,hc->ghp", key_rows, probe_heads, preferred_element_type=jnp.float32)
        * root_scale
    )
    weights = jax.nn.softmax(scores, axis=-1)
    weights_low = weights.astype(jnp.bfloat16)
    heads_out = jnp.einsum(
        "ghp,gphc->ghc", weights_low, value_rows, preferred_element_type=jnp.float32
    )
    heads_out = heads_out.astype(jnp.bfloat16).reshape(group, local_width)
    partial_out = jnp.dot(heads_out, w_out, preferred_element_type=jnp.float32)
    row_loss, text_grad, group_grad = loss_call(nz, nn, partial_out.reshape(nn, ROWS, D), texts)
    head_grad = jnp.dot(group_grad, w_out.T, preferred_element_type=jnp.float32).reshape(
        group, local_heads, HEAD_DIM
    )
    out_term = lax.dot_general(
        group_grad, heads_out, (((0,), (0,)), ((), ())), preferred_element_type=jnp.float32
    )
    value_grad = jnp.einsum("ghp,ghc->gphc", weights_low.astype(jnp.float32), head_grad).astype(
        jnp.bfloat16
    )
    weight_grad = jnp.einsum(
        "ghc,gphc->ghp", head_grad, value_rows, precision=lax.Precision.HIGHEST
    )
    score_grad = weights * (weight_grad - jnp.sum(weights * weight_grad, axis=-1, keepdims=True))
    key_grad = (
        jnp.einsum("ghp,hc->gphc", score_grad, probe_heads.astype(jnp.float32)) * root_scale
    ).astype(jnp.bfloat16)
    both_grad = jnp.concatenate(
        [
            key_grad.reshape(group * PATCHES, local_width),
            value_grad.reshape(group * PATCHES, local_width),
        ],
        axis=1,
    )
    kv_term = lax.dot_general(
        flat_rows, both_grad, (((0,), (0,)), ((), ())), preferred_element_type=jnp.float32
    )
    half = 256
    first = kv_term[:, :half]
    second = jnp.concatenate(
        [kv_term[:, half:], out_term, jnp.zeros((D, 2 * half - 3 * local_width), jnp.float32)], axis=1
    )
    grads = jnp.stack([first, second]).reshape(2, nz, D // nz, half)
    total = sum_call(nz, grads)
    return (
        row_loss[:, 0],
        text_grad,
        total[:, :local_width],
        total[:, local_width : 2 * local_width],
        total[:, 2 * local_width : 3 * local_width].T,
    )


def solution(mesh):
    return jax.shard_map(
        shards,
        mesh=mesh,
        in_specs=(
            P("wide", None, None),
            P(None, "narrow"),
            P(None, "narrow"),
            P("narrow", None),
            P("narrow"),
            P(("wide", "narrow"), None),
        ),
        out_specs=(
            P(("wide", "narrow")),
            P(("wide", "narrow"), None),
            P("wide", "narrow"),
            P("wide", "narrow"),
            P("narrow", "wide"),
        ),
        check_vma=False,
    )
```

time: 771 us -> 125 us (0.16); the launches traced: 762 us -> 125 us
  waiting for transfers between devices: 507 us -> 0 us
  blocking collectives: 152 us -> 0 us
  Pallas kernels: 0 us -> 75.7 us
  between operations: 17.3 us -> 0.84 us
  matrix products: 46.4 us -> 30 us
  starting transfers between devices: 13.3 us -> 0 us
    unnamed x10 -> x0, waiting for transfers between devices: 443 us -> none
    unnamed x1 -> x0, blocking collectives: 82.5 us -> none
    pallas_call x0 -> x2, Pallas kernels: none -> 75.7 us  [the longest x1 38.9 us: sum_call(): pl.pallas_call(functools.partial(sum_kernel, nz), out_shape=jax.ShapeDtyp...]
    all_gather x2 -> x0, blocking collectives: 69.8 us -> none  [the longest x1 47 us: shards(): text_group = lax.all_gather(text_low, 'wide', axis=0, tiled=True)]
    ppermute x15 -> x0, waiting for transfers between devices: 64.5 us -> none  [passed_along(): return lax.ppermute(block, axis, route)]
    dot_general x25 -> x1, matrix products: 11.9 us -> 0.3 us  [shards(): lax.dot_general(group_grad, heads_out, (((0,), (0,)), ((), ())), preferre...]
    unnamed x7 -> x0, starting transfers between devices: 9.58 us -> none
  transfers between devices with their start and end apart: 22 -> 0, of which waited for: 18 -> 0; matrix products, arithmetic and copies ran while one was open for 17% -> 0% of each run, Pallas kernels for 0% -> 0%
where the time goes in v1:
time: 125 us
  Pallas kernels  75.7 us (61%)
  matrix products  30 us (24%)
  local copies, waits for them, and re-layouts  14.9 us (12%)
  other arithmetic  3.51 us (3%)
    pallas_call x1, Pallas kernels, sum_call(): pl.pallas_call(functools.partial(sum_kernel, nz), out_shape=jax.ShapeDtyp...  38.9 us
    pallas_call x1, Pallas kernels, loss_call(): pl.pallas_call(functools.partial(loss_kernel, nz, nn), out_shape=(jax.Sha...  36.7 us
    dot_general x1, matrix products, shards(): lax.dot_general(flat_rows, both_grad, (((0,), (0,)), ((), ())), preferred...  10.9 us
    dot_general x1, matrix products, shards(): jnp.dot(flat_rows, w_both, preferred_element_type=jnp.float32)  10.5 us
    unnamed x13, local copies, waits for them, and re-layouts  7.96 us
    dot_general x1, matrix products, shards(): jnp.einsum('ghc,gphc->ghp', head_grad, value_rows, precision=lax.Precisio...  3.98 us
    slice x2, local copies, waits for them, and re-layouts, shards(): first = kv_term[:, :half]  2.73 us
    dot_general x1, matrix products, shards(): jnp.einsum('ghp,gphc->ghc', weights_low, value_rows, preferred_element_ty...  2.6 us

profile of v1, /device:TPU:1, one launch (start us, length us, event | category | flops | bytes accessed | tf_op | source)
XLA Modules:
  0.0 124.9 jit_solution(17395051615845684060)
XLA Ops:
  0.6 0.0 copy-start
  0.6 10.5 %fusion.3 = bf16[8192,288]{0,1:T(8,128)(2,1)S(1)} fusion(bf16[8192,1152]{1,0:T(8,128)(2,1)} %bitcast.86, bf16[1152,144]{0,1:T(8,128)(2,1)} %param.8, bf16[1152,144]{0,1:T(8,128)(2,1)} %param.7), kind=kOutput, calls=%fused_computation.4 | convolution fusion | flops 5439504384 | bytes 24256512 | tf_op jit(solution)/shard_map/dot_general | solution.py:265
  11.2 1.8 %fusion.41 = (bf16[8192,144]{0,1:T(8,128)(2,1)S(1)}, bf16[8192,144]{0,1:T(8,128)(2,1)}) fusion(bf16[8192,288]{0,1:T(8,128)(2,1)S(1)} %fusion.3), kind=kLoop, calls=%fused_computation.48 | loop fusion | bytes 9437184 | tf_op jit(solution)/shard_map/slice | solution.py:266
  13.0 0.0 copy-start.3
  13.0 0.7 copy.31
  13.7 0.0 copy-done.3
  13.7 0.1 reshape.61
  13.8 1.4 %fusion.11 = f32[2,1,32,256]{3,1,2,0:T(1,128)S(1)} fusion(bf16[2,72,1,1]{1,2,3,0:T(2,128)(2,1)S(1)} %reshape.61, bf16[32,256,2,72]{1,0,3,2:T(8,128)(2,1)S(1)} %bitcast.81), kind=kOutput, calls=%fused_computation.13 | convolution fusion | flops 2359296 | bytes 2425120 | tf_op jit(solution)/shard_map/gphc,hc->ghp/dot_general | solution.py:269
  15.1 0.2 fusion.18
  15.3 2.4 %copy.32 = bf16[18,8,32,256]{3,2,1,0:T(8,128)(2,1)S(1)} copy(bf16[18,8,32,256]{3,1,2,0:T(8,128)(2,1)} %bitcast.76) | data formatting | bytes 4718592
  17.7 0.0 copy-start.1
  17.7 2.6 %fusion.15 = f32[32,2,1,72]{3,2,1,0:T(1,128)S(1)} fusion(bf16[32,256,2,72]{1,0,3,2:T(8,128)(2,1)S(1)} %bitcast.72, bf16[32,2,256,1]{2,0,1,3:T(8,128)(2,1)S(1)} %get-tuple-element.17), kind=kOutput, calls=%fused_computation.17 | convolution fusion | flops 2359296 | bytes 2410496 | tf_op jit(solution)/shard_map/ghp,gphc->ghc/dot_general | solution.py:274
  20.3 0.1 dot_general.45
  20.4 0.0 copy-done
  20.4 0.2 fusion.26.partial
  20.6 0.0 copy-done.1
  20.6 36.7 %shard_map.101 = (f32[4,128]{1,0:T(4,128)S(1)}, f32[4,1152]{1,0:T(4,128)S(1)}, bf16[32,1152]{1,0:T(8,128)(2,1)S(1)}) custom-call(f32[8,4,1152]{2,1,0:T(4,128)S(1)} %fusion.26.partial, bf16[4,1152]{1,0:T(4,128)(2,1)S(1)} %copy-done.1), custom_call_target="tpu_custom_call" | custom-call | tf_op jit(solution)/shard_map/pallas_call | solution.py:155
  57.3 0.2 fusion.42
  57.5 0.2 reshape.58
  57.7 4.0 %fusion.13 = f32[32,2,1,256]{3,2,1,0:T(1,128)S(1)} fusion(f32[32,2,72,1]{2,3,1,0:T(1,128)S(1)} %bitcast.84, bf16[32,256,2,72]{1,0,3,2:T(8,128)(2,1)S(1)} %bitcast.73), kind=kOutput, calls=%fused_computation.15 | convolution fusion | flops 14155776 | bytes 2443264 | tf_op jit(solution)/shard_map/ghc,gphc->ghp/dot_general | solution.py:289
  61.6 0.3 fusion.22
  62.0 0.1 reshape.47
  62.1 0.5 multiply_convert_fusion.1
  62.6 1.6 %copy.33 = bf16[18,8,32,256]{3,1,2,0:T(8,128)(2,1)S(1)} copy(bf16[18,8,32,256]{3,2,1,0:T(8,128)(2,1)S(1)} %bitcast.74) | data formatting | bytes 4718592
  64.2 0.1 copy.30
  64.3 0.8 multiply_convert_fusion
  65.1 1.6 %copy.34 = bf16[18,8,32,256]{3,1,2,0:T(8,128)(2,1)S(1)} copy(bf16[18,8,32,256]{3,2,1,0:T(8,128)(2,1)S(1)} %bitcast.75) | data formatting | bytes 4718592
  66.7 10.9 %fusion.8 = f32[1152,288]{0,1:T(8,128)S(1)} fusion(bf16[8192,1152]{1,0:T(8,128)(2,1)} %bitcast.87, bf16[8192,144]{0,1:T(8,128)(2,1)S(1)} %bitcast.82, bf16[8192,144]{0,1:T(8,128)(2,1)S(1)} %bitcast.80), kind=kOutput, calls=%fused_computation.11 | convolution fusion | flops 5445255168 | bytes 24920064 | tf_op jit(solution)/shard_map/dot_general | solution.py:303
  77.6 0.0 copy-start.2
  77.6 1.1 copy-done.2
  78.7 0.1 reshape.52
  78.8 0.3 fusion.43
  79.1 0.1 pad.4.clone
  79.2 0.1 maximum_maximum_fusion
  79.4 0.4 copy.19
  79.7 1.3 %slice.34 = f32[1152,256]{0,1:T(8,128)S(1)} slice(f32[1152,288]{0,1:T(8,128)} %copy-done.2), slice={[0:1152], [0:256]} | slice | bytes 2359296 | tf_op jit(solution)/shard_map/slice | solution.py:307
  81.1 1.4 %copy.18 = f32[1152,256]{1,0:T(8,128)} copy(f32[1152,256]{0,1:T(8,128)S(1)} %slice.34) | data formatting | bytes 2359296 | tf_op jit(solution)/shard_map/slice | solution.py:307
  82.5 1.6 %pad_maximum_fusion.grads = f32[2,8,144,256]{3,2,1,0:T(8,128)S(1)} fusion(f32[1,8,144,256]{3,2,1,0:T(8,128)S(1)} %bitcast.78, f32[1,8,144,256]{3,2,1,0:T(8,128)} %bitcast.79), kind=kLoop, calls=%fused_computation.12 | loop fusion | flops 589824 | bytes 4718592 | tf_op jit(solution)/shard_map/stack | solution.py:311
  84.0 38.9 %shard_map.102 = f32[36,512]{1,0:T(8,128)S(1)} custom-call(f32[2,8,144,256]{3,2,1,0:T(8,128)S(1)} %pad_maximum_fusion.grads), custom_call_target="tpu_custom_call" | custom-call | tf_op jit(solution)/shard_map/pallas_call | solution.py:231
  123.0 0.7 slice_bitcast_fusion
  123.7 0.6 slice_reduce_fusion
  124.3 0.6 copy.57
  (5 shorter events, 0.0 us)
Async XLA Ops:
  0.6 19.8 %copy-start = (bf16[144,1152]{1,0:T(8,128)(2,1)S(1)}, bf16[144,1152]{1,0:T(8,128)(2,1)}, u32[]{:S(2)}) copy-start(bf16[144,1152]{1,0:T(8,128)(2,1)} %param.9) | copy-start | bytes 995332
  13.0 0.7 copy-start.3
  17.7 2.9 %copy-start.1 = (bf16[4,1152]{1,0:T(4,128)(2,1)S(1)}, bf16[4,1152]{1,0:T(4,128)(2,1)}, u32[]{:S(2)}) copy-start(bf16[4,1152]{1,0:T(4,128)(2,1)} %texts.1) | copy-start | bytes 27652
  77.6 1.1 copy-start.2

commit v2 on v1

v2 whole, which is shorter than its diff:
```python
import functools
import math

import jax
import jax.numpy as jnp
from jax import lax
from jax.experimental import pallas as pl
from jax.experimental.pallas import tpu as pltpu
from jax.sharding import PartitionSpec as P

D = 1152
HEAD_DIM = 72
PATCHES = 256
QUAD = 4
ROWS = 4
MESH = pl.DeviceIdType.MESH

logit_scale = 16.0
logit_bias = -4.0


def remote(src, dst, send, recv, device):
    copy = pltpu.make_async_remote_copy(
        src_ref=src,
        dst_ref=dst,
        send_sem=send,
        recv_sem=recv,
        device_id=device,
        device_id_type=MESH,
    )
    copy.start()
    return copy


def split_dot(coef, other, dims):
    high = coef.astype(jnp.bfloat16)
    rest = coef - high.astype(jnp.float32)
    mid = rest.astype(jnp.bfloat16)
    low = (rest - mid.astype(jnp.float32)).astype(jnp.bfloat16)
    dot = lambda part: lax.dot_general(part, other, dims, preferred_element_type=jnp.float32)
    return dot(low) + dot(mid) + dot(high)


CHUNK = 4
SPAN = CHUNK * PATCHES
SLOTS = 2 * CHUNK
WIDTH = 384
NT = (((1,), (1,)), ((), ()))
NN = (((1,), (0,)), ((), ()))


def matmul(a, b, dims=NN):
    return lax.dot_general(a, b, dims, preferred_element_type=jnp.float32)


def high_low(values):
    high = values.astype(jnp.bfloat16)
    low = (values - high.astype(jnp.float32)).astype(jnp.bfloat16)
    return high, low


def iota(shape, axis):
    return lax.broadcasted_iota(jnp.int32, shape, axis)


def kernel(
    nz, nn, patches, w_key, w_value, w_out, probe, texts,
    loss_out, text_out, key_out, value_out, out_out,
    held, both_t, keys, values, weights, heads, pooled_rows, left,
    psrc, rbuf, qbuf, tbuf, ibuf, gsrc, gbuf, usrc, ubuf, vsrc, vbuf, pbuf,
    grads, abuf, xsrc, xbuf, zsrc, zbuf, head_rows, ssum, sbuf, szsum, szbuf,
    loads, nsend, nrecv, zsend, zrecv, qsend, qrecv, asend, arecv, xsend, xrecv,
):
    f32, bf16 = jnp.float32, jnp.bfloat16
    w, n = lax.axis_index("wide"), lax.axis_index("narrow")
    z, q = w // QUAD, lax.rem(w, QUAD)
    x, core = q // 2, lax.rem(q, 2)
    group, span = nn * ROWS, nz * QUAD * ROWS
    chunks = group // CHUNK
    width = w_key.shape[1]
    root_scale = 1.0 / math.sqrt(HEAD_DIM)
    narrow_peers = [lax.rem(n + d, nn) for d in range(1, nn)]
    z_peers = [lax.rem(z + d, nz) for d in range(1, nz)]
    q_peers = [lax.rem(q + d, QUAD) for d in range(1, QUAD)]
    at_n = lambda k: {"wide": w, "narrow": k}
    at_z = lambda k: {"wide": k * QUAD + q, "narrow": n}
    at_q = lambda k: {"wide": z * QUAD + k, "narrow": n}
    sibling = at_q(q + 1 - 2 * core)
    across = at_q(2 * (1 - x) + core)
    order = z_peers + [z]

    for j in range(chunks):
        pltpu.make_async_copy(patches.at[pl.ds(j * SPAN, SPAN)], held.at[j], loads.at[j]).start()
    barrier = pltpu.get_barrier_semaphore()
    partners = [at_n(k) for k in narrow_peers] + [at_z(k) for k in z_peers] + [at_q(k) for k in q_peers]
    for device in partners:
        pl.semaphore_signal(barrier, inc=1, device_id=device, device_id_type=MESH)
    sent = []

    def exchange(peers, place, me, src, dst, send, recv):
        copies = [remote(src(k), dst.at[me], send.at[k], recv.at[me], place(k)) for k in peers]
        sent.extend(copies)

    def arrived(peers, buf, recv):
        for k in peers:
            pltpu.make_async_copy(buf.at[k], buf.at[k], recv.at[k]).wait()

    both_t[:width] = w_key[...].T
    both_t[width:] = w_value[...].T
    slot_head = iota((SLOTS, width), 0) // CHUNK
    lane_head = iota((SLOTS, width), 1) // HEAD_DIM
    probe_row = probe[...].astype(f32)
    probe_slots = jnp.where(slot_head == lane_head, probe_row, 0.0).astype(bf16)
    slot_image = iota((SLOTS, SPAN), 0) % CHUNK
    own = slot_image == iota((SLOTS, SPAN), 1) // PATCHES

    def project(j, slot):
        pltpu.make_async_copy(held.at[j], held.at[j], loads.at[j]).wait()
        rows = matmul(both_t[...], held[j], NT).astype(bf16)
        keys[slot] = rows[:width]
        values[j] = rows[width:]

    def pool(j, slot):
        scores = matmul(probe_slots, keys[slot]) * root_scale
        scores = jnp.where(own, scores, -1e30)
        top = jnp.max(scores, axis=1, keepdims=True)
        shifted = jnp.where(own, jnp.exp(scores - top), 0.0)
        part = shifted / jnp.sum(shifted, axis=1, keepdims=True)
        weights[j] = part
        heads[j] = matmul(part.astype(bf16), values[j], NT)

    project(0, 0)

    def step(j, carry):
        project(j, lax.rem(j, 2))
        pool(j - 1, lax.rem(j + 1, 2))
        return carry

    first, second = chunks // 2, chunks - 2
    lax.fori_loop(1, first, step, 0)
    pl.semaphore_wait(barrier, len(partners))
    text_float = texts[...].astype(f32)
    text_norm = jnp.sqrt(jnp.sum(text_float * text_float, axis=1, keepdims=True) + 1e-06)
    text_unit = text_float / text_norm
    qbuf[q] = text_unit.astype(bf16).astype(f32)
    exchange(q_peers, at_q, q, lambda k: qbuf.at[q], qbuf, qsend.at[0], qrecv.at[0])
    lax.fori_loop(first, second, step, 0)
    arrived(q_peers, qbuf, qrecv.at[0])
    tbuf[z] = jnp.concatenate([qbuf[k] for k in range(QUAD)], axis=0).astype(bf16)
    exchange(z_peers, at_z, z, lambda k: tbuf.at[z], tbuf, zsend.at[0], zrecv.at[0])
    lax.fori_loop(second, chunks, step, 0)
    pool(chunks - 1, (chunks - 1) % 2)

    all_slots = chunks * SLOTS
    slot_of = iota((all_slots, width), 0)
    head_mask = (slot_of % SLOTS) // CHUNK == iota((all_slots, width), 1) // HEAD_DIM
    heads_slots = jnp.where(head_mask, heads[...].reshape(all_slots, width), 0.0).astype(bf16)
    row_of = iota((group, all_slots), 0)
    slot_at = iota((group, all_slots), 1)
    gather = jnp.where(slot_at // SLOTS * CHUNK + slot_at % CHUNK == row_of, 1.0, 0.0).astype(bf16)
    heads_out = matmul(gather, heads_slots).astype(bf16)
    partial = matmul(heads_out, w_out[...])
    for k in range(nn):
        psrc[k] = partial[k * ROWS : (k + 1) * ROWS]
    exchange(narrow_peers, at_n, n, lambda k: psrc.at[k], rbuf, nsend.at[0], nrecv.at[0])

    def pool_rows(first, last):
        for j in range(first, last):
            rows = matmul(weights[j].astype(bf16), held[j])
            pooled_rows[j * SLOTS : (j + 1) * SLOTS] = rows

    half = chunks // 2
    pool_rows(0, half)
    arrived(narrow_peers, rbuf, nrecv.at[0])
    pooled = psrc[n]
    for k in narrow_peers:
        pooled = pooled + rbuf[k]
    pooled_norm = jnp.sqrt(jnp.sum(pooled * pooled, axis=1, keepdims=True) + 1e-06)
    image_unit = pooled / pooled_norm
    ibuf[n] = image_unit.astype(bf16).astype(f32)
    exchange(narrow_peers, at_n, n, lambda k: ibuf.at[n], ibuf, nsend.at[1], nrecv.at[1])
    pool_rows(half, chunks)
    arrived(z_peers, tbuf, zrecv.at[0])
    arrived(narrow_peers, ibuf, nrecv.at[1])

    image_low = jnp.concatenate([ibuf[k] for k in range(nn)], axis=0).astype(bf16)
    text_low = tbuf[...].reshape(span, D)
    logits = logit_scale * matmul(image_low, text_low, NT) + logit_bias
    image_ids = w * group + iota((group, span), 0)
    offsets = iota((group, span), 1)
    text_ids = offsets // ROWS * group + n * ROWS + offsets % ROWS
    signs = jnp.where(image_ids == text_ids, 1.0, -1.0).astype(f32)
    margin = -signs * logits
    small = jnp.exp(-jnp.abs(margin))
    loss_part = jnp.sum(jnp.maximum(margin, 0.0) + jnp.log1p(small), axis=1, keepdims=True)
    coef = -signs * jnp.where(margin >= 0.0, 1.0, small) / (1.0 + small)
    image_part = logit_scale * split_dot(coef, text_low, NN)
    for k in range(nn):
        gsrc[k, :, :D] = image_part[k * ROWS : (k + 1) * ROWS]
        gsrc[k, :, D:] = jnp.broadcast_to(loss_part[k * ROWS : (k + 1) * ROWS], (ROWS, 128))
    exchange(narrow_peers, at_n, n, lambda k: gsrc.at[k], gbuf, nsend.at[2], nrecv.at[2])
    text_part = logit_scale * split_dot(coef.T, image_low, NN)
    usrc[...] = text_part.astype(bf16).reshape(nz, QUAD * ROWS, D)
    exchange(z_peers, at_z, z, lambda k: usrc.at[k], ubuf, zsend.at[1], zrecv.at[1])
    high, low = high_low(pooled_rows[...])
    pooled_t = jnp.concatenate([high, low, high], axis=0).T
    blocks = D // nz
    for k in range(nz):
        left[k, :, : 3 * all_slots] = pooled_t[k * blocks : (k + 1) * blocks]

    arrived(narrow_peers, gbuf, nrecv.at[2])
    both = gsrc[n]
    for k in narrow_peers:
        both = both + gbuf[k]
    loss_out[...] = both[:, D:]
    image_grad = both[:, :D]
    pooled_grad = (
        image_grad - image_unit * jnp.sum(image_unit * image_grad, axis=1, keepdims=True)
    ) / pooled_norm
    pbuf[n] = pooled_grad.astype(bf16).astype(f32)
    exchange(narrow_peers, at_n, n, lambda k: pbuf.at[n], pbuf, nsend.at[3], nrecv.at[3])

    arrived(z_peers, ubuf, zrecv.at[1])
    quad_grad = usrc[z].astype(f32)
    for k in z_peers:
        quad_grad = quad_grad + ubuf[k].astype(f32)
    for k in range(QUAD):
        vsrc[k] = quad_grad[k * ROWS : (k + 1) * ROWS]
    exchange(q_peers, at_q, q, lambda k: vsrc.at[k], vbuf, qsend.at[1], qrecv.at[1])

    arrived(narrow_peers, pbuf, nrecv.at[3])
    group_float = jnp.concatenate([pbuf[k] for k in range(nn)], axis=0)
    group_grad = group_float.astype(bf16)
    scatter = jnp.where(
        iota((all_slots, group), 0) // SLOTS * CHUNK + iota((all_slots, group), 0) % CHUNK
        == iota((all_slots, group), 1),
        1.0,
        0.0,
    ).astype(bf16)
    slot_grads = matmul(scatter, group_grad).astype(bf16)
    head_grad = jnp.where(head_mask, matmul(slot_grads, w_out[...], NT), 0.0)
    high = head_grad.astype(bf16).astype(f32)
    low = head_grad - high
    none = lambda rows, columns: jnp.zeros((rows, columns), f32)
    spare = 4 * all_slots - 3 * all_slots - group
    turned = jnp.concatenate([group_float, none(spare, D)], axis=0).astype(bf16).T
    for k in range(nz):
        left[k, :, 3 * all_slots :] = turned[k * blocks : (k + 1) * blocks]

    def value_rows(part):
        return jnp.concatenate(
            [part[:, :128], none(all_slots, 128), part[:, 128:], none(all_slots, 112)], axis=1
        )

    heads_float = heads_out.astype(f32)
    out_rows = jnp.concatenate(
        [none(group, 128), heads_float[:, :128], none(group, 16), heads_float[:, 128:], none(group, 96)],
        axis=1,
    )
    right = jnp.concatenate(
        [value_rows(high), value_rows(high), value_rows(low), out_rows, none(spare, WIDTH)], axis=0
    ).astype(bf16)
    rows = blocks // QUAD
    for k in order:
        block = matmul(left[k], right)
        for there in range(QUAD):
            grads[k, there % 2, there // 2] = block[there * rows : (there + 1) * rows]
        sent.append(remote(grads.at[k, 1 - core], abuf.at[k], asend.at[k], arecv.at[k], sibling))
    for j in range(chunks):
        pair = [high[j * SLOTS : (j + 1) * SLOTS], low[j * SLOTS : (j + 1) * SLOTS]]
        head_rows[j] = jnp.concatenate(pair, axis=0).astype(bf16)

    score_sum = none(2 * SLOTS, D)
    for j in range(chunks):
        weight_grad = matmul(head_rows[j], values[j])
        weight_grad = weight_grad[:SLOTS] + weight_grad[SLOTS:]
        part = weights[j]
        inner = jnp.sum(part * weight_grad, axis=1, keepdims=True)
        score_grad = part * (weight_grad - inner)
        top = score_grad.astype(bf16).astype(f32)
        pair = jnp.concatenate([top, score_grad - top], axis=0).astype(bf16)
        score_sum = score_sum + matmul(pair, held[j])
    per_head = score_sum[:SLOTS] + score_sum[SLOTS:]
    for h in range(2):
        ssum[h : h + 1] = jnp.sum(per_head[h * CHUNK : (h + 1) * CHUNK], axis=0, keepdims=True)
    sbuf[q] = ssum[...]
    exchange(q_peers, at_q, q, lambda k: ssum, sbuf, qsend.at[2], qrecv.at[2])

    for k in order:
        pltpu.make_async_copy(abuf.at[k], abuf.at[k], arecv.at[k]).wait()
        xsrc[k] = grads[k, core, 1 - x] + abuf[k, 1 - x]
        sent.append(remote(xsrc.at[k], xbuf.at[k], xsend.at[k], xrecv.at[k], across))
    arrived(q_peers, sbuf, qrecv.at[2])
    szsum[...] = sbuf[0] + sbuf[1] + sbuf[2] + sbuf[3]
    exchange(z_peers, at_z, z, lambda k: szsum, szbuf, zsend.at[2], zrecv.at[2])
    for i, k in enumerate(order):
        pltpu.make_async_copy(xbuf.at[k], xbuf.at[k], xrecv.at[k]).wait()
        total = grads[k, core, x] + abuf[k, x] + xbuf[k]
        if i < nz - 1:
            zsrc[k] = total
            sent.append(remote(zsrc.at[k], zbuf.at[z], zsend.at[3, k], zrecv.at[3, z], at_z(k)))

    arrived(q_peers, vbuf, qrecv.at[1])
    unit_grad = vsrc[q]
    for k in q_peers:
        unit_grad = unit_grad + vbuf[k]
    text_out[...] = (
        unit_grad - text_unit * jnp.sum(text_unit * unit_grad, axis=1, keepdims=True)
    ) / text_norm

    arrived(z_peers, szbuf, zrecv.at[2])
    scores_all = szsum[...]
    for k in z_peers:
        scores_all = scores_all + szbuf[k]
    one = scores_all.astype(bf16).astype(f32)
    two = (scores_all - one).astype(bf16).astype(f32)
    three = scores_all - one - two
    parts = jnp.concatenate([one, two, three, none(2, D)], axis=0).astype(bf16)
    pick = jnp.where(iota((rows, D), 0) + w * rows == iota((rows, D), 1), 1.0, 0.0).astype(bf16)
    picked = matmul(pick, parts, NT)
    first_head = picked[:, 0:1] + picked[:, 2:3] + picked[:, 4:5]
    second_head = picked[:, 1:2] + picked[:, 3:4] + picked[:, 5:6]
    by_head = jnp.where(iota((rows, width), 1) < HEAD_DIM, first_head, second_head)
    key_out[...] = by_head * probe_row * root_scale

    for k in reversed(z_peers):
        pltpu.make_async_copy(zbuf.at[k], zbuf.at[k], zrecv.at[3, k]).wait()
        total = total + zbuf[k]
    value_out[...] = jnp.concatenate([total[:, :128], total[:, 256:272]], axis=1)
    out_out[...] = jnp.concatenate([total[:, 128:256], total[:, 272:288]], axis=1)
    for copy in sent:
        copy.wait_send()


def call(nz, nn, patches, w_key, w_value, w_out, probe, texts):
    vmem = pl.BlockSpec(memory_space=pltpu.VMEM)
    f32, bf16 = jnp.float32, jnp.bfloat16
    group = nn * ROWS
    chunks = group // CHUNK
    width = w_key.shape[1]
    rows = D // nz // QUAD
    slots = chunks * SLOTS
    dma = pltpu.SemaphoreType.DMA
    return pl.pallas_call(
        functools.partial(kernel, nz, nn),
        out_shape=(
            jax.ShapeDtypeStruct((ROWS, 128), f32),
            jax.ShapeDtypeStruct((ROWS, D), f32),
            jax.ShapeDtypeStruct((rows, width), f32),
            jax.ShapeDtypeStruct((rows, width), f32),
            jax.ShapeDtypeStruct((rows, width), f32),
        ),
        in_specs=[pl.BlockSpec(memory_space=pl.ANY)] + [vmem] * 5,
        out_specs=(vmem,) * 5,
        scratch_shapes=[
            pltpu.VMEM((chunks, SPAN, D), bf16),
            pltpu.VMEM((2 * width, D), bf16),
            pltpu.VMEM((2, width, SPAN), bf16),
            pltpu.VMEM((chunks, width, SPAN), bf16),
            pltpu.VMEM((chunks, SLOTS, SPAN), f32),
            pltpu.VMEM((chunks, SLOTS, width), f32),
            pltpu.VMEM((slots, D), f32),
            pltpu.VMEM((nz, D // nz, 4 * slots), bf16),
            pltpu.VMEM((nn, ROWS, D), f32),
            pltpu.VMEM((nn, ROWS, D), f32),
            pltpu.VMEM((QUAD, ROWS, D), f32),
            pltpu.VMEM((nz, QUAD * ROWS, D), bf16),
            pltpu.VMEM((nn, ROWS, D), f32),
            pltpu.VMEM((nn, ROWS, D + 128), f32),
            pltpu.VMEM((nn, ROWS, D + 128), f32),
            pltpu.VMEM((nz, QUAD * ROWS, D), bf16),
            pltpu.VMEM((nz, QUAD * ROWS, D), bf16),
            pltpu.VMEM((QUAD, ROWS, D), f32),
            pltpu.VMEM((QUAD, ROWS, D), f32),
            pltpu.VMEM((nn, ROWS, D), f32),
            pltpu.VMEM((nz, 2, 2, rows, WIDTH), f32),
            pltpu.VMEM((nz, 2, rows, WIDTH), f32),
            pltpu.VMEM((nz, rows, WIDTH), f32),
            pltpu.VMEM((nz, rows, WIDTH), f32),
            pltpu.VMEM((nz, rows, WIDTH), f32),
            pltpu.VMEM((nz, rows, WIDTH), f32),
            pltpu.VMEM((chunks, 2 * SLOTS, width), bf16),
            pltpu.VMEM((2, D), f32),
            pltpu.VMEM((QUAD, 2, D), f32),
            pltpu.VMEM((2, D), f32),
            pltpu.VMEM((nz, 2, D), f32),
            dma((chunks,)),
            dma((4, nn)),
            dma((4, nn)),
            dma((4, nz)),
            dma((4, nz)),
            dma((3, QUAD)),
            dma((3, QUAD)),
            dma((nz,)),
            dma((nz,)),
            dma((nz,)),
            dma((nz,)),
        ],
        compiler_params=pltpu.CompilerParams(
            collective_id=0, has_side_effects=True, vmem_limit_bytes=56 * 1024 * 1024
        ),
    )(patches, w_key, w_value, w_out, probe, texts)


def shards(patches, w_key, w_value, w_out, probe, texts):
    nz = lax.axis_size("wide") // QUAD
    nn = lax.axis_size("narrow")
    flat_rows = patches.reshape(patches.shape[0] * PATCHES, D)
    row_loss, text_grad, grad_key, grad_value, grad_out = call(
        nz, nn, flat_rows, w_key, w_value, w_out, probe.reshape(1, -1), texts
    )
    return (row_loss[:, 0], text_grad, grad_key, grad_value, grad_out.T)


def solution(mesh):
    return jax.shard_map(
        shards,
        mesh=mesh,
        in_specs=(
            P("wide", None, None),
            P(None, "narrow"),
            P(None, "narrow"),
            P("narrow", None),
            P("narrow"),
            P(("wide", "narrow"), None),
        ),
        out_specs=(
            P(("wide", "narrow")),
            P(("wide", "narrow"), None),
            P("wide", "narrow"),
            P("wide", "narrow"),
            P("narrow", "wide"),
        ),
        check_vma=False,
    )
```

time: 125 us -> 81.3 us (0.65); the launches traced: 125 us -> 79.9 us
  matrix products: 30 us -> 0 us
  Pallas kernels: 75.7 us -> 67.1 us
  other arithmetic: 3.51 us -> 0 us
  local copies, waits for them, and re-layouts: 14.9 us -> 12.1 us
    dot_general x8 -> x0, matrix products: 30 us -> none  [the longest x1 10.9 us: shards(): lax.dot_general(flat_rows, both_grad, (((0,), (0,)), ((), ())), preferred...]
    pallas_call x2 -> x1, Pallas kernels: 75.7 us -> 67.1 us  [call(): pl.pallas_call(functools.partial(kernel, nz, nn), out_shape=(jax.ShapeDty...]
    slice x5 -> x1, local copies, waits for them, and re-layouts: 5.15 us -> 1.31 us  [shards(): return (row_loss[:, 0], text_grad, grad_key, grad_value, grad_out.T)]
    unnamed x13 -> x6, local copies, waits for them, and re-layouts: 7.96 us -> 9.56 us
    another operation x3 -> x0, other arithmetic: 1.59 us -> none  [the longest x1 1.57 us: shards(): grads = jnp.stack([first, second]).reshape(2, nz, D // nz, half)]
    convert_element_type x3 -> x0, other arithmetic: 1.26 us -> none  [the longest x1 0.78 us: shards(): jnp.einsum('ghp,ghc->gphc', weights_low.astype(jnp.float32), head_grad)]
where the time goes in v2:
time: 81.3 us; the launch traced here: 79.9 us
  Pallas kernels  67.1 us (83%)
  local copies, waits for them, and re-layouts  12.1 us (15%)
    pallas_call x1, Pallas kernels, call(): pl.pallas_call(functools.partial(kernel, nz, nn), out_shape=(jax.ShapeDty...  67.1 us
    unnamed x6, local copies, waits for them, and re-layouts  9.56 us

profile of v2, /device:TPU:1, one launch (start us, length us, event | category | flops | bytes accessed | tf_op | source)
XLA Modules:
  0.0 79.9 jit_solution(16380576978175742616)
XLA Ops:
  0.6 1.2 %reshape.17.probe = bf16[1,144]{1,0:T(2,128)(2,1)} reshape(bf16[144]{0:T(256)(128)(2,1)} %param.10) | data formatting | bytes 576 | tf_op jit(solution)/shard_map/reshape | solution.py:410
  1.9 2.0 %copy.13.w_key = bf16[1152,144]{1,0:T(8,128)(2,1)} copy(bf16[1152,144]{0,1:T(8,128)(2,1)} %param.7) | data formatting | bytes 663552 | tf_op args[1]
  3.9 2.0 %copy.14.w_value = bf16[1152,144]{1,0:T(8,128)(2,1)} copy(bf16[1152,144]{0,1:T(8,128)(2,1)} %param.8) | data formatting | bytes 663552 | tf_op args[2]
  5.9 67.1 %shard_map.101 = (f32[4,128]{1,0:T(4,128)}, f32[4,1152]{1,0:T(4,128)}, f32[36,144]{1,0:T(8,128)}, f32[36,144]{1,0:T(8,128)}, f32[36,144]{1,0:T(8,128)}) custom-call(bf16[8192,1152]{1,0:T(8,128)(2,1)} %bitcast.2, bf16[1152,144]{1,0:T(8,128)(2,1)} %copy.13.w_key, bf16[1152,144]{1,0:T(8,128)(2,1)} %copy.14.w_value, bf16[144,1152]{1,0:T(8,128)(2,1)} %w_out.1, ...), custom_call_target="tpu_custom_call" | custom-call | tf_op jit(solution)/shard_map/pallas_call | solution.py:344
  73.0 1.3 %slice_reduce_fusion = f32[4]{0:T(128)} fusion(f32[4,128]{1,0:T(4,128)} %get-tuple-element.10), kind=kLoop, calls=%fused_computation | loop fusion | bytes 32 | tf_op jit(solution)/shard_map/slice | solution.py:412
  74.3 1.3 %copy.19 = f32[4,1152]{1,0:T(4,128)} copy(f32[4,1152]{1,0:T(4,128)} %get-tuple-element.21) | data formatting | bytes 36864
  75.7 1.4 %copy.20 = f32[36,144]{1,0:T(8,128)} copy(f32[36,144]{1,0:T(8,128)} %get-tuple-element.22) | data formatting | bytes 41472
  77.1 1.4 %copy.21 = f32[36,144]{1,0:T(8,128)} copy(f32[36,144]{1,0:T(8,128)} %get-tuple-element.23) | data formatting | bytes 41472
  78.5 1.4 %copy.22 = f32[144,36]{0,1:T(8,128)} copy(f32[144,36]{0,1:T(8,128)} %bitcast.3) | data formatting | bytes 41472

commit v3 on v2

--- a/solution.py
+++ b/solution.py
@@ -66,7 +66,7 @@
 def kernel(
     nz, nn, patches, w_key, w_value, w_out, probe, texts,
     loss_out, text_out, key_out, value_out, out_out,
-    held, both_t, keys, values, weights, heads, pooled_rows, left,
+    held, both_t, out_w, keys, values, weights, heads, pooled_rows, left,
     psrc, rbuf, qbuf, tbuf, ibuf, gsrc, gbuf, usrc, ubuf, vsrc, vbuf, pbuf,
     grads, abuf, xsrc, xbuf, zsrc, zbuf, head_rows, ssum, sbuf, szsum, szbuf,
     loads, nsend, nrecv, zsend, zrecv, qsend, qrecv, asend, arecv, xsend, xrecv,
@@ -77,7 +77,7 @@
     x, core = q // 2, lax.rem(q, 2)
     group, span = nn * ROWS, nz * QUAD * ROWS
     chunks = group // CHUNK
-    width = w_key.shape[1]
+    width = w_key.shape[0]
     root_scale = 1.0 / math.sqrt(HEAD_DIM)
     narrow_peers = [lax.rem(n + d, nn) for d in range(1, nn)]
     z_peers = [lax.rem(z + d, nz) for d in range(1, nz)]
@@ -89,12 +89,18 @@
     across = at_q(2 * (1 - x) + core)
     order = z_peers + [z]
 
-    for j in range(chunks):
-        pltpu.make_async_copy(patches.at[pl.ds(j * SPAN, SPAN)], held.at[j], loads.at[j]).start()
     barrier = pltpu.get_barrier_semaphore()
     partners = [at_n(k) for k in narrow_peers] + [at_z(k) for k in z_peers] + [at_q(k) for k in q_peers]
     for device in partners:
         pl.semaphore_signal(barrier, inc=1, device_id=device, device_id_type=MESH)
+    key_load = pltpu.make_async_copy(w_key, both_t.at[pl.ds(0, width)], loads.at[chunks])
+    value_load = pltpu.make_async_copy(w_value, both_t.at[pl.ds(width, width)], loads.at[chunks + 1])
+    out_load = pltpu.make_async_copy(w_out, out_w, loads.at[chunks + 2])
+    key_load.start()
+    value_load.start()
+    for j in range(chunks):
+        pltpu.make_async_copy(patches.at[pl.ds(j * SPAN, SPAN)], held.at[j], loads.at[j]).start()
+    out_load.start()
     sent = []
 
     def exchange(peers, place, me, src, dst, send, recv):
@@ -105,23 +111,27 @@
         for k in peers:
             pltpu.make_async_copy(buf.at[k], buf.at[k], recv.at[k]).wait()
 
-    both_t[:width] = w_key[...].T
-    both_t[width:] = w_value[...].T
+    text_float = texts[...].astype(f32)
+    text_norm = jnp.sqrt(jnp.sum(text_float * text_float, axis=1, keepdims=True) + 1e-06)
+    text_unit = text_float / text_norm
+    qbuf[q] = text_unit.astype(bf16).astype(f32)
+    pl.semaphore_wait(barrier, len(partners))
+    exchange(q_peers, at_q, q, lambda k: qbuf.at[q], qbuf, qsend.at[0], qrecv.at[0])
     slot_head = iota((SLOTS, width), 0) // CHUNK
     lane_head = iota((SLOTS, width), 1) // HEAD_DIM
-    probe_row = probe[...].astype(f32)
+    probe_row = probe[...].reshape(1, width).astype(f32)
     probe_slots = jnp.where(slot_head == lane_head, probe_row, 0.0).astype(bf16)
     slot_image = iota((SLOTS, SPAN), 0) % CHUNK
     own = slot_image == iota((SLOTS, SPAN), 1) // PATCHES
 
-    def project(j, slot):
+    def project(j):
         pltpu.make_async_copy(held.at[j], held.at[j], loads.at[j]).wait()
         rows = matmul(both_t[...], held[j], NT).astype(bf16)
-        keys[slot] = rows[:width]
+        keys[j] = rows[:width]
         values[j] = rows[width:]
 
-    def pool(j, slot):
-        scores = matmul(probe_slots, keys[slot]) * root_scale
+    def pool(j):
+        scores = matmul(probe_slots, keys[j]) * root_scale
         scores = jnp.where(own, scores, -1e30)
         top = jnp.max(scores, axis=1, keepdims=True)
         shifted = jnp.where(own, jnp.exp(scores - top), 0.0)
@@ -129,27 +139,16 @@
         weights[j] = part
         heads[j] = matmul(part.astype(bf16), values[j], NT)
 
-    project(0, 0)
-
-    def step(j, carry):
-        project(j, lax.rem(j, 2))
-        pool(j - 1, lax.rem(j + 1, 2))
-        return carry
-
-    first, second = chunks // 2, chunks - 2
-    lax.fori_loop(1, first, step, 0)
-    pl.semaphore_wait(barrier, len(partners))
-    text_float = texts[...].astype(f32)
-    text_norm = jnp.sqrt(jnp.sum(text_float * text_float, axis=1, keepdims=True) + 1e-06)
-    text_unit = text_float / text_norm
-    qbuf[q] = text_unit.astype(bf16).astype(f32)
-    exchange(q_peers, at_q, q, lambda k: qbuf.at[q], qbuf, qsend.at[0], qrecv.at[0])
-    lax.fori_loop(first, second, step, 0)
+    key_load.wait()
+    value_load.wait()
+    project(0)
     arrived(q_peers, qbuf, qrecv.at[0])
     tbuf[z] = jnp.concatenate([qbuf[k] for k in range(QUAD)], axis=0).astype(bf16)
     exchange(z_peers, at_z, z, lambda k: tbuf.at[z], tbuf, zsend.at[0], zrecv.at[0])
-    lax.fori_loop(second, chunks, step, 0)
-    pool(chunks - 1, (chunks - 1) % 2)
+    for j in range(1, chunks):
+        project(j)
+    for j in range(chunks):
+        pool(j)
 
     all_slots = chunks * SLOTS
     slot_of = iota((all_slots, width), 0)
@@ -159,7 +158,8 @@
     slot_at = iota((group, all_slots), 1)
     gather = jnp.where(slot_at // SLOTS * CHUNK + slot_at % CHUNK == row_of, 1.0, 0.0).astype(bf16)
     heads_out = matmul(gather, heads_slots).astype(bf16)
-    partial = matmul(heads_out, w_out[...])
+    out_load.wait()
+    partial = matmul(heads_out, out_w[...])
     for k in range(nn):
         psrc[k] = partial[k * ROWS : (k + 1) * ROWS]
     exchange(narrow_peers, at_n, n, lambda k: psrc.at[k], rbuf, nsend.at[0], nrecv.at[0])
@@ -212,21 +212,15 @@
     both = gsrc[n]
     for k in narrow_peers:
         both = both + gbuf[k]
-    loss_out[...] = both[:, D:]
+    diagonal = iota((ROWS, 128), 0) == iota((ROWS, 128), 1)
+    losses = jnp.sum(jnp.where(diagonal, both[:, D:], 0.0), axis=0, keepdims=True)
+    loss_out[...] = losses[:, :ROWS]
     image_grad = both[:, :D]
     pooled_grad = (
         image_grad - image_unit * jnp.sum(image_unit * image_grad, axis=1, keepdims=True)
     ) / pooled_norm
     pbuf[n] = pooled_grad.astype(bf16).astype(f32)
     exchange(narrow_peers, at_n, n, lambda k: pbuf.at[n], pbuf, nsend.at[3], nrecv.at[3])
-
-    arrived(z_peers, ubuf, zrecv.at[1])
-    quad_grad = usrc[z].astype(f32)
-    for k in z_peers:
-        quad_grad = quad_grad + ubuf[k].astype(f32)
-    for k in range(QUAD):
-        vsrc[k] = quad_grad[k * ROWS : (k + 1) * ROWS]
-    exchange(q_peers, at_q, q, lambda k: vsrc.at[k], vbuf, qsend.at[1], qrecv.at[1])
 
     arrived(narrow_peers, pbuf, nrecv.at[3])
     group_float = jnp.concatenate([pbuf[k] for k in range(nn)], axis=0)
@@ -238,7 +232,7 @@
         0.0,
     ).astype(bf16)
     slot_grads = matmul(scatter, group_grad).astype(bf16)
-    head_grad = jnp.where(head_mask, matmul(slot_grads, w_out[...], NT), 0.0)
+    head_grad = jnp.where(head_mask, matmul(slot_grads, out_w[...], NT), 0.0)
     high = head_grad.astype(bf16).astype(f32)
     low = head_grad - high
     none = lambda rows, columns: jnp.zeros((rows, columns), f32)
@@ -261,16 +255,28 @@
         [value_rows(high), value_rows(high), value_rows(low), out_rows, none(spare, WIDTH)], axis=0
     ).astype(bf16)
     rows = blocks // QUAD
+    fold = rows // 4
     for k in order:
         block = matmul(left[k], right)
         for there in range(QUAD):
-            grads[k, there % 2, there // 2] = block[there * rows : (there + 1) * rows]
+            part = block[there * rows : (there + 1) * rows]
+            here = grads.at[k, there % 2, there // 2]
+            here[:rows] = part[:, :128]
+            here[rows : 2 * rows] = part[:, 128:256]
+            pieces = [part[g * fold : (g + 1) * fold, 256:288] for g in range(4)]
+            here[2 * rows :] = jnp.concatenate(pieces, axis=1)
         sent.append(remote(grads.at[k, 1 - core], abuf.at[k], asend.at[k], arecv.at[k], sibling))
     for j in range(chunks):
         pair = [high[j * SLOTS : (j + 1) * SLOTS], low[j * SLOTS : (j + 1) * SLOTS]]
         head_rows[j] = jnp.concatenate(pair, axis=0).astype(bf16)
 
+    def forward(k):
+        pltpu.make_async_copy(abuf.at[k], abuf.at[k], arecv.at[k]).wait()
+        xsrc[k] = grads[k, core, 1 - x] + abuf[k, 1 - x]
+        sent.append(remote(xsrc.at[k], xbuf.at[k], xsend.at[k], xrecv.at[k], across))
+
     score_sum = none(2 * SLOTS, D)
+    passed = 0
     for j in range(chunks):
         weight_grad = matmul(head_rows[j], values[j])
         weight_grad = weight_grad[:SLOTS] + weight_grad[SLOTS:]
@@ -280,16 +286,25 @@
         top = score_grad.astype(bf16).astype(f32)
         pair = jnp.concatenate([top, score_grad - top], axis=0).astype(bf16)
         score_sum = score_sum + matmul(pair, held[j])
+        if j % 2 == 1:
+            upto = nz * (j + 1) // chunks
+            for k in order[passed:upto]:
+                forward(k)
+            passed = upto
     per_head = score_sum[:SLOTS] + score_sum[SLOTS:]
     for h in range(2):
         ssum[h : h + 1] = jnp.sum(per_head[h * CHUNK : (h + 1) * CHUNK], axis=0, keepdims=True)
     sbuf[q] = ssum[...]
     exchange(q_peers, at_q, q, lambda k: ssum, sbuf, qsend.at[2], qrecv.at[2])
 
-    for k in order:
-        pltpu.make_async_copy(abuf.at[k], abuf.at[k], arecv.at[k]).wait()
-        xsrc[k] = grads[k, core, 1 - x] + abuf[k, 1 - x]
-        sent.append(remote(xsrc.at[k], xbuf.at[k], xsend.at[k], xrecv.at[k], across))
+    arrived(z_peers, ubuf, zrecv.at[1])
+    quad_grad = usrc[z].astype(f32)
+    for k in z_peers:
+        quad_grad = quad_grad + ubuf[k].astype(f32)
+    for k in range(QUAD):
+        vsrc[k] = quad_grad[k * ROWS : (k + 1) * ROWS]
+    exchange(q_peers, at_q, q, lambda k: vsrc.at[k], vbuf, qsend.at[1], qrecv.at[1])
+
     arrived(q_peers, sbuf, qrecv.at[2])
     szsum[...] = sbuf[0] + sbuf[1] + sbuf[2] + sbuf[3]
     exchange(z_peers, at_z, z, lambda k: szsum, szbuf, zsend.at[2], zrecv.at[2])
@@ -326,10 +341,36 @@
     for k in reversed(z_peers):
         pltpu.make_async_copy(zbuf.at[k], zbuf.at[k], zrecv.at[3, k]).wait()
         total = total + zbuf[k]
-    value_out[...] = jnp.concatenate([total[:, :128], total[:, 256:272]], axis=1)
-    out_out[...] = jnp.concatenate([total[:, 128:256], total[:, 272:288]], axis=1)
+    rest = total[2 * rows :]
+    rest = jnp.concatenate([rest[:, 32 * g : 32 * (g + 1)] for g in range(4)], axis=0)
+    value_out[...] = jnp.concatenate([total[:rows], rest[:, :16]], axis=1)
+    out_out[...] = jnp.concatenate([total[rows : 2 * rows], rest[:, 16:]], axis=1)
     for copy in sent:
         copy.wait_send()
+
+
+def finish_kernel(*refs):
+    count = len(refs) // 2
+    sems = refs[-1]
+    copies = [
+        pltpu.make_async_copy(refs[k], refs[count + k], sems.at[k]) for k in range(count)
+    ]
+    for copy in copies:
+        copy.start()
+    for copy in copies:
+        copy.wait()
+
+
+def finish(*arrays):
+    anywhere = pl.BlockSpec(memory_space=pl.ANY)
+    return pl.pallas_call(
+        finish_kernel,
+        out_shape=tuple(jax.ShapeDtypeStruct(a.shape, a.dtype) for a in arrays),
+        in_specs=[anywhere] * len(arrays),
+        out_specs=(anywhere,) * len(arrays),
+        scratch_shapes=[pltpu.SemaphoreType.DMA((len(arrays),))],
+        compiler_params=pltpu.CompilerParams(vmem_limit_bytes=60 * 1024 * 1024),
+    )(*arrays)
 
 
 def call(nz, nn, patches, w_key, w_value, w_out, probe, texts):
@@ -337,25 +378,27 @@
     f32, bf16 = jnp.float32, jnp.bfloat16
     group = nn * ROWS
     chunks = group // CHUNK
-    width = w_key.shape[1]
+    width = w_key.shape[0]
     rows = D // nz // QUAD
+    slab = 2 * rows + rows // 4
     slots = chunks * SLOTS
     dma = pltpu.SemaphoreType.DMA
     return pl.pallas_call(
         functools.partial(kernel, nz, nn),
         out_shape=(
-            jax.ShapeDtypeStruct((ROWS, 128), f32),
+            jax.ShapeDtypeStruct((1, ROWS), f32),
             jax.ShapeDtypeStruct((ROWS, D), f32),
             jax.ShapeDtypeStruct((rows, width), f32),
             jax.ShapeDtypeStruct((rows, width), f32),
             jax.ShapeDtypeStruct((rows, width), f32),
         ),
-        in_specs=[pl.BlockSpec(memory_space=pl.ANY)] + [vmem] * 5,
+        in_specs=[pl.BlockSpec(memory_space=pl.ANY)] * 4 + [vmem] * 2,
         out_specs=(vmem,) * 5,
         scratch_shapes=[
             pltpu.VMEM((chunks, SPAN, D), bf16),
             pltpu.VMEM((2 * width, D), bf16),
-            pltpu.VMEM((2, width, SPAN), bf16),
+            pltpu.VMEM((width, D), bf16),
+            pltpu.VMEM((chunks, width, SPAN), bf16),
             pltpu.VMEM((chunks, width, SPAN), bf16),
             pltpu.VMEM((chunks, SLOTS, SPAN), f32),
             pltpu.VMEM((chunks, SLOTS, width), f32),
@@ -373,18 +416,18 @@
             pltpu.VMEM((QUAD, ROWS, D), f32),
             pltpu.VMEM((QUAD, ROWS, D), f32),
             pltpu.VMEM((nn, ROWS, D), f32),
-            pltpu.VMEM((nz, 2, 2, rows, WIDTH), f32),
-            pltpu.VMEM((nz, 2, rows, WIDTH), f32),
-            pltpu.VMEM((nz, rows, WIDTH), f32),
-            pltpu.VMEM((nz, rows, WIDTH), f32),
-            pltpu.VMEM((nz, rows, WIDTH), f32),
-            pltpu.VMEM((nz, rows, WIDTH), f32),
+            pltpu.VMEM((nz, 2, 2, slab, 128), f32),
+            pltpu.VMEM((nz, 2, slab, 128), f32),
+            pltpu.VMEM((nz, slab, 128), f32),
+            pltpu.VMEM((nz, slab, 128), f32),
+            pltpu.VMEM((nz, slab, 128), f32),
+            pltpu.VMEM((nz, slab, 128), f32),
             pltpu.VMEM((chunks, 2 * SLOTS, width), bf16),
             pltpu.VMEM((2, D), f32),
             pltpu.VMEM((QUAD, 2, D), f32),
             pltpu.VMEM((2, D), f32),
             pltpu.VMEM((nz, 2, D), f32),
-            dma((chunks,)),
+            dma((chunks + 3,)),
             dma((4, nn)),
             dma((4, nn)),
             dma((4, nz)),
@@ -407,9 +450,12 @@
     nn = lax.axis_size("narrow")
     flat_rows = patches.reshape(patches.shape[0] * PATCHES, D)
     row_loss, text_grad, grad_key, grad_value, grad_out = call(
-        nz, nn, flat_rows, w_key, w_value, w_out, probe.reshape(1, -1), texts
+        nz, nn, flat_rows, w_key.T, w_value.T, w_out, probe, texts
     )
-    return (row_loss[:, 0], text_grad, grad_key, grad_value, grad_out.T)
+    row_loss, text_grad, grad_key, grad_value, grad_out = finish(
+        row_loss, text_grad, grad_key, grad_value, grad_out
+    )
+    return (row_loss.reshape(ROWS), text_grad, grad_key, grad_value, grad_out.T)
 
 
 def solution(mesh):

time: 81.3 us -> 73.8 us (0.908); the launches traced: 79.9 us -> 73.7 us
  local copies, waits for them, and re-layouts: 12.1 us -> 0 us
  Pallas kernels: 67.1 us -> 73 us
    unnamed x6 -> x0, local copies, waits for them, and re-layouts: 9.56 us -> none
    pallas_call x0 -> x1, Pallas kernels: none -> 5.45 us  [finish(): pl.pallas_call(finish_kernel, out_shape=tuple((jax.ShapeDtypeStruct(a.sha...]
    slice x1 -> x0, local copies, waits for them, and re-layouts: 1.31 us -> none  [shards(): return (row_loss[:, 0], text_grad, grad_key, grad_value, grad_out.T)]
    reshape x1 -> x0, local copies, waits for them, and re-layouts: 1.22 us -> none  [shards(): probe.reshape(1, -1)]
where the time goes in v3:
time: 73.8 us; the launch traced here: 73.7 us
  Pallas kernels  73 us (99%)
    pallas_call x1, Pallas kernels, call(): pl.pallas_call(functools.partial(kernel, nz, nn), out_shape=(jax.ShapeDty...  67.6 us
    pallas_call x1, Pallas kernels, finish(): pl.pallas_call(finish_kernel, out_shape=tuple((jax.ShapeDtypeStruct(a.sha...  5.45 us

profile of v3, /device:TPU:1, one launch (start us, length us, event | category | flops | bytes accessed | tf_op | source)
XLA Modules:
  0.0 73.7 jit_solution(9344006813606251487)
XLA Ops:
  0.6 67.6 %shard_map.101 = (f32[1,4]{1,0:T(1,128)}, f32[4,1152]{1,0:T(4,128)}, f32[36,144]{1,0:T(8,128)}, f32[36,144]{1,0:T(8,128)}, f32[36,144]{1,0:T(8,128)}) custom-call(bf16[8192,1152]{1,0:T(8,128)(2,1)} %bitcast.5, bf16[144,1152]{1,0:T(8,128)(2,1)} %bitcast.6, bf16[144,1152]{1,0:T(8,128)(2,1)} %bitcast.7, bf16[144,1152]{1,0:T(8,128)(2,1)} %w_out.1, ...), custom_call_target="tpu_custom_call" | custom-call | tf_op jit(solution)/shard_map/pallas_call | solution.py:386
  68.2 5.4 %shard_map.102 = (f32[1,4]{1,0:T(1,128)}, f32[4,1152]{1,0:T(4,128)}, f32[36,144]{1,0:T(8,128)}, f32[36,144]{1,0:T(8,128)}, f32[36,144]{1,0:T(8,128)}) custom-call(f32[1,4]{1,0:T(1,128)} %get-tuple-element.15.refs_0_, f32[4,1152]{1,0:T(4,128)} %get-tuple-element.16.refs_1_, f32[36,144]{1,0:T(8,128)} %get-tuple-element.17.refs_2_, ...), custom_call_target="tpu_custom_call" | custom-call | tf_op jit(solution)/shard_map/pallas_call | solution.py:366

commit v4 on v3

--- a/solution.py
+++ b/solution.py
@@ -35,10 +35,9 @@
 def split_dot(coef, other, dims):
     high = coef.astype(jnp.bfloat16)
     rest = coef - high.astype(jnp.float32)
-    mid = rest.astype(jnp.bfloat16)
-    low = (rest - mid.astype(jnp.float32)).astype(jnp.bfloat16)
+    low = rest.astype(jnp.bfloat16)
     dot = lambda part: lax.dot_general(part, other, dims, preferred_element_type=jnp.float32)
-    return dot(low) + dot(mid) + dot(high)
+    return dot(low) + dot(high)
 
 
 CHUNK = 4
@@ -255,6 +254,7 @@
         [value_rows(high), value_rows(high), value_rows(low), out_rows, none(spare, WIDTH)], axis=0
     ).astype(bf16)
     rows = blocks // QUAD
+    slab = zsrc.shape[1]
     fold = rows // 4
     for k in order:
         block = matmul(left[k], right)
@@ -272,11 +272,22 @@
 
     def forward(k):
         pltpu.make_async_copy(abuf.at[k], abuf.at[k], arecv.at[k]).wait()
-        xsrc[k] = grads[k, core, 1 - x] + abuf[k, 1 - x]
+        given = grads[k, core, 1 - x] + abuf[k, 1 - x]
+        given = jnp.concatenate([given, none(xsrc.shape[1] - slab, 128)], axis=0)
+        xsrc[k] = given.astype(bf16)
         sent.append(remote(xsrc.at[k], xbuf.at[k], xsend.at[k], xrecv.at[k], across))
 
+    def onward(i):
+        k = order[i]
+        pltpu.make_async_copy(xbuf.at[k], xbuf.at[k], xrecv.at[k]).wait()
+        total = grads[k, core, x] + abuf[k, x] + xbuf[k].astype(f32)[:slab]
+        if i < nz - 1:
+            zsrc[k] = total
+            sent.append(remote(zsrc.at[k], zbuf.at[z], zsend.at[3, k], zrecv.at[3, z], at_z(k)))
+        return total
+
     score_sum = none(2 * SLOTS, D)
-    passed = 0
+    passed, moved = 0, 0
     for j in range(chunks):
         weight_grad = matmul(head_rows[j], values[j])
         weight_grad = weight_grad[:SLOTS] + weight_grad[SLOTS:]
@@ -286,16 +297,21 @@
         top = score_grad.astype(bf16).astype(f32)
         pair = jnp.concatenate([top, score_grad - top], axis=0).astype(bf16)
         score_sum = score_sum + matmul(pair, held[j])
-        if j % 2 == 1:
-            upto = nz * (j + 1) // chunks
-            for k in order[passed:upto]:
-                forward(k)
-            passed = upto
+        upto = nz * j // (chunks - 1)
+        for k in order[passed:upto]:
+            forward(k)
+        passed = upto
+        while moved < passed - 4:
+            onward(moved)
+            moved += 1
     per_head = score_sum[:SLOTS] + score_sum[SLOTS:]
     for h in range(2):
         ssum[h : h + 1] = jnp.sum(per_head[h * CHUNK : (h + 1) * CHUNK], axis=0, keepdims=True)
     sbuf[q] = ssum[...]
     exchange(q_peers, at_q, q, lambda k: ssum, sbuf, qsend.at[2], qrecv.at[2])
+    while moved < nz:
+        total = onward(moved)
+        moved += 1
 
     arrived(z_peers, ubuf, zrecv.at[1])
     quad_grad = usrc[z].astype(f32)
@@ -308,13 +324,6 @@
     arrived(q_peers, sbuf, qrecv.at[2])
     szsum[...] = sbuf[0] + sbuf[1] + sbuf[2] + sbuf[3]
     exchange(z_peers, at_z, z, lambda k: szsum, szbuf, zsend.at[2], zrecv.at[2])
-    for i, k in enumerate(order):
-        pltpu.make_async_copy(xbuf.at[k], xbuf.at[k], xrecv.at[k]).wait()
-        total = grads[k, core, x] + abuf[k, x] + xbuf[k]
-        if i < nz - 1:
-            zsrc[k] = total
-            sent.append(remote(zsrc.at[k], zbuf.at[z], zsend.at[3, k], zrecv.at[3, z], at_z(k)))
-
     arrived(q_peers, vbuf, qrecv.at[1])
     unit_grad = vsrc[q]
     for k in q_peers:
@@ -351,24 +360,17 @@
 
 def finish_kernel(*refs):
     count = len(refs) // 2
-    sems = refs[-1]
-    copies = [
-        pltpu.make_async_copy(refs[k], refs[count + k], sems.at[k]) for k in range(count)
-    ]
-    for copy in copies:
-        copy.start()
-    for copy in copies:
-        copy.wait()
+    for source, target in zip(refs[:count], refs[count:]):
+        target[...] = source[...]
 
 
 def finish(*arrays):
-    anywhere = pl.BlockSpec(memory_space=pl.ANY)
+    vmem = pl.BlockSpec(memory_space=pltpu.VMEM)
     return pl.pallas_call(
         finish_kernel,
         out_shape=tuple(jax.ShapeDtypeStruct(a.shape, a.dtype) for a in arrays),
-        in_specs=[anywhere] * len(arrays),
-        out_specs=(anywhere,) * len(arrays),
-        scratch_shapes=[pltpu.SemaphoreType.DMA((len(arrays),))],
+        in_specs=[vmem] * len(arrays),
+        out_specs=(vmem,) * len(arrays),
         compiler_params=pltpu.CompilerParams(vmem_limit_bytes=60 * 1024 * 1024),
     )(*arrays)
 
@@ -381,6 +383,7 @@
     width = w_key.shape[0]
     rows = D // nz // QUAD
     slab = 2 * rows + rows // 4
+    wire = -(-slab // 16) * 16
     slots = chunks * SLOTS
     dma = pltpu.SemaphoreType.DMA
     return pl.pallas_call(
@@ -418,8 +421,8 @@
             pltpu.VMEM((nn, ROWS, D), f32),
             pltpu.VMEM((nz, 2, 2, slab, 128), f32),
             pltpu.VMEM((nz, 2, slab, 128), f32),
-            pltpu.VMEM((nz, slab, 128), f32),
-            pltpu.VMEM((nz, slab, 128), f32),
+            pltpu.VMEM((nz, wire, 128), bf16),
+            pltpu.VMEM((nz, wire, 128), bf16),
             pltpu.VMEM((nz, slab, 128), f32),
             pltpu.VMEM((nz, slab, 128), f32),
             pltpu.VMEM((chunks, 2 * SLOTS, width), bf16),

time: 73.8 us -> 64.8 us (0.88)
  Pallas kernels: 73 us -> 64 us
    pallas_call x1, Pallas kernels: 67.6 us -> 62.5 us  [call(): pl.pallas_call(functools.partial(kernel, nz, nn), out_shape=(jax.ShapeDty...]
    pallas_call x1, Pallas kernels: 5.45 us -> 1.5 us  [finish(): pl.pallas_call(finish_kernel, out_shape=tuple((jax.ShapeDtypeStruct(a.sha...]
where the time goes in v4:
time: 64.8 us; the launch traced here: 64.7 us
  Pallas kernels  64 us (99%)
    pallas_call x1, Pallas kernels, call(): pl.pallas_call(functools.partial(kernel, nz, nn), out_shape=(jax.ShapeDty...  62.5 us
    pallas_call x1, Pallas kernels, finish(): pl.pallas_call(finish_kernel, out_shape=tuple((jax.ShapeDtypeStruct(a.sha...  1.5 us

profile of v4, /device:TPU:1, one launch (start us, length us, event | category | flops | bytes accessed | tf_op | source)
XLA Modules:
  0.0 64.7 jit_solution(5825989171687560992)
XLA Ops:
  0.6 62.5 %shard_map.101 = (f32[1,4]{1,0:T(1,128)}, f32[4,1152]{1,0:T(4,128)}, f32[36,144]{1,0:T(8,128)}, f32[36,144]{1,0:T(8,128)}, f32[36,144]{1,0:T(8,128)}) custom-call(bf16[8192,1152]{1,0:T(8,128)(2,1)} %bitcast.5, bf16[144,1152]{1,0:T(8,128)(2,1)} %bitcast.6, bf16[144,1152]{1,0:T(8,128)(2,1)} %bitcast.7, bf16[144,1152]{1,0:T(8,128)(2,1)} %w_out.1, ...), custom_call_target="tpu_custom_call" | custom-call | tf_op jit(solution)/shard_map/pallas_call | solution.py:389
  63.2 1.5 %shard_map.102 = (f32[1,4]{1,0:T(1,128)}, f32[4,1152]{1,0:T(4,128)}, f32[36,144]{1,0:T(8,128)}, f32[36,144]{1,0:T(8,128)}, f32[36,144]{1,0:T(8,128)}) custom-call(f32[1,4]{1,0:T(1,128)} %get-tuple-element.15.refs_0_, f32[4,1152]{1,0:T(4,128)} %get-tuple-element.16.refs_1_, f32[36,144]{1,0:T(8,128)} %get-tuple-element.17.refs_2_, ...), custom_call_target="tpu_custom_call" | custom-call | tf_op jit(solution)/shard_map/pallas_call | solution.py:369

commit v5 on v4

--- a/solution.py
+++ b/solution.py
@@ -67,7 +67,7 @@
     loss_out, text_out, key_out, value_out, out_out,
     held, both_t, out_w, keys, values, weights, heads, pooled_rows, left,
     psrc, rbuf, qbuf, tbuf, ibuf, gsrc, gbuf, usrc, ubuf, vsrc, vbuf, pbuf,
-    grads, abuf, xsrc, xbuf, zsrc, zbuf, head_rows, ssum, sbuf, szsum, szbuf,
+    grads, abuf, xsrc, xbuf, zsrc, zbuf, osrc, obuf, pick, head_rows, ssum, sbuf, szsum, szbuf,
     loads, nsend, nrecv, zsend, zrecv, qsend, qrecv, asend, arecv, xsend, xrecv,
 ):
     f32, bf16 = jnp.float32, jnp.bfloat16
@@ -140,12 +140,12 @@
 
     key_load.wait()
     value_load.wait()
-    project(0)
-    arrived(q_peers, qbuf, qrecv.at[0])
-    tbuf[z] = jnp.concatenate([qbuf[k] for k in range(QUAD)], axis=0).astype(bf16)
-    exchange(z_peers, at_z, z, lambda k: tbuf.at[z], tbuf, zsend.at[0], zrecv.at[0])
-    for j in range(1, chunks):
+    for j in range(chunks):
         project(j)
+        if j == 1:
+            arrived(q_peers, qbuf, qrecv.at[0])
+            tbuf[z] = jnp.concatenate([qbuf[k] for k in range(QUAD)], axis=0).astype(bf16)
+            exchange(z_peers, at_z, z, lambda k: tbuf.at[z], tbuf, zsend.at[0], zrecv.at[0])
     for j in range(chunks):
         pool(j)
 
@@ -170,6 +170,11 @@
 
     half = chunks // 2
     pool_rows(0, half)
+    each = D // (nz * QUAD)
+    for k in range(nz):
+        lane = iota((D, 128), 1)
+        chosen = (iota((D, 128), 0) == (k * QUAD + q) * each + lane) & (lane < each)
+        pick[:, k * 128 : (k + 1) * 128] = jnp.where(chosen, 1.0, 0.0).astype(bf16)
     arrived(narrow_peers, rbuf, nrecv.at[0])
     pooled = psrc[n]
     for k in narrow_peers:
@@ -254,26 +259,25 @@
         [value_rows(high), value_rows(high), value_rows(low), out_rows, none(spare, WIDTH)], axis=0
     ).astype(bf16)
     rows = blocks // QUAD
-    slab = zsrc.shape[1]
+    wide = zsrc.shape[1]
+    slab = wide + rows
     fold = rows // 4
-    for k in order:
+    def block_out(k):
         block = matmul(left[k], right)
         for there in range(QUAD):
             part = block[there * rows : (there + 1) * rows]
             here = grads.at[k, there % 2, there // 2]
             here[:rows] = part[:, :128]
-            here[rows : 2 * rows] = part[:, 128:256]
             pieces = [part[g * fold : (g + 1) * fold, 256:288] for g in range(4)]
-            here[2 * rows :] = jnp.concatenate(pieces, axis=1)
+            pieces = jnp.concatenate(pieces, axis=1)
+            here[rows:wide] = jnp.concatenate([pieces, none(wide - rows - fold, 128)], axis=0)
+            here[wide:] = part[:, 128:256]
         sent.append(remote(grads.at[k, 1 - core], abuf.at[k], asend.at[k], arecv.at[k], sibling))
-    for j in range(chunks):
-        pair = [high[j * SLOTS : (j + 1) * SLOTS], low[j * SLOTS : (j + 1) * SLOTS]]
-        head_rows[j] = jnp.concatenate(pair, axis=0).astype(bf16)
 
     def forward(k):
         pltpu.make_async_copy(abuf.at[k], abuf.at[k], arecv.at[k]).wait()
         given = grads[k, core, 1 - x] + abuf[k, 1 - x]
-        given = jnp.concatenate([given, none(xsrc.shape[1] - slab, 128)], axis=0)
+        given = jnp.concatenate([given, none(2 * wide - slab, 128)], axis=0)
         xsrc[k] = given.astype(bf16)
         sent.append(remote(xsrc.at[k], xbuf.at[k], xsend.at[k], xrecv.at[k], across))
 
@@ -282,12 +286,29 @@
         pltpu.make_async_copy(xbuf.at[k], xbuf.at[k], xrecv.at[k]).wait()
         total = grads[k, core, x] + abuf[k, x] + xbuf[k].astype(f32)[:slab]
         if i < nz - 1:
-            zsrc[k] = total
+            zsrc[k] = total[:wide]
             sent.append(remote(zsrc.at[k], zbuf.at[z], zsend.at[3, k], zrecv.at[3, z], at_z(k)))
+            osrc[k] = jnp.concatenate([total[wide:], none(2 * wide - slab, 128)], axis=0).astype(bf16)
+            sent.append(remote(osrc.at[k], obuf.at[z], zsend.at[4, k], zrecv.at[4, z], at_z(k)))
         return total
 
+    for i in range(nz):
+        block_out(order[i])
+        if i > 1:
+            forward(order[i - 2])
+    for j in range(chunks):
+        pair = [high[j * SLOTS : (j + 1) * SLOTS], low[j * SLOTS : (j + 1) * SLOTS]]
+        head_rows[j] = jnp.concatenate(pair, axis=0).astype(bf16)
+    forward(order[nz - 2])
+    forward(order[nz - 1])
+
+    def three_parts(values):
+        one = values.astype(bf16).astype(f32)
+        two = (values - one).astype(bf16).astype(f32)
+        return jnp.concatenate([one, two, values - one - two, jnp.zeros_like(one)], axis=0).astype(bf16)
+
     score_sum = none(2 * SLOTS, D)
-    passed, moved = 0, 0
+    moved = 0
     for j in range(chunks):
         weight_grad = matmul(head_rows[j], values[j])
         weight_grad = weight_grad[:SLOTS] + weight_grad[SLOTS:]
@@ -297,13 +318,10 @@
         top = score_grad.astype(bf16).astype(f32)
         pair = jnp.concatenate([top, score_grad - top], axis=0).astype(bf16)
         score_sum = score_sum + matmul(pair, held[j])
-        upto = nz * j // (chunks - 1)
-        for k in order[passed:upto]:
-            forward(k)
-        passed = upto
-        while moved < passed - 4:
-            onward(moved)
-            moved += 1
+        if j > 0:
+            while moved < nz * j // chunks:
+                total = onward(moved)
+                moved += 1
     per_head = score_sum[:SLOTS] + score_sum[SLOTS:]
     for h in range(2):
         ssum[h : h + 1] = jnp.sum(per_head[h * CHUNK : (h + 1) * CHUNK], axis=0, keepdims=True)
@@ -322,8 +340,12 @@
     exchange(q_peers, at_q, q, lambda k: vsrc.at[k], vbuf, qsend.at[1], qrecv.at[1])
 
     arrived(q_peers, sbuf, qrecv.at[2])
-    szsum[...] = sbuf[0] + sbuf[1] + sbuf[2] + sbuf[3]
-    exchange(z_peers, at_z, z, lambda k: szsum, szbuf, zsend.at[2], zrecv.at[2])
+    scores_all = sbuf[0] + sbuf[1] + sbuf[2] + sbuf[3]
+    picked = matmul(three_parts(scores_all), pick[...])
+    for k in range(nz):
+        mine = picked[:, k * 128 : (k + 1) * 128]
+        szsum[k] = mine[0:2] + mine[2:4] + mine[4:6]
+    exchange(z_peers, at_z, z, lambda k: szsum.at[k], szbuf, zsend.at[2], zrecv.at[2])
     arrived(q_peers, vbuf, qrecv.at[1])
     unit_grad = vsrc[q]
     for k in q_peers:
@@ -333,27 +355,25 @@
     ) / text_norm
 
     arrived(z_peers, szbuf, zrecv.at[2])
-    scores_all = szsum[...]
+    scores_all = szsum[z]
     for k in z_peers:
         scores_all = scores_all + szbuf[k]
-    one = scores_all.astype(bf16).astype(f32)
-    two = (scores_all - one).astype(bf16).astype(f32)
-    three = scores_all - one - two
-    parts = jnp.concatenate([one, two, three, none(2, D)], axis=0).astype(bf16)
-    pick = jnp.where(iota((rows, D), 0) + w * rows == iota((rows, D), 1), 1.0, 0.0).astype(bf16)
-    picked = matmul(pick, parts, NT)
-    first_head = picked[:, 0:1] + picked[:, 2:3] + picked[:, 4:5]
-    second_head = picked[:, 1:2] + picked[:, 3:4] + picked[:, 5:6]
-    by_head = jnp.where(iota((rows, width), 1) < HEAD_DIM, first_head, second_head)
-    key_out[...] = by_head * probe_row * root_scale
-
+    spread = jnp.where(
+        (iota((8, width), 0) % 2 == iota((8, width), 1) // HEAD_DIM) & (iota((8, width), 0) < 6), probe_row, 0.0
+    ).astype(bf16)
+    keyed = matmul(three_parts(scores_all), spread, (((0,), (0,)), ((), ())))
+    key_out[...] = keyed[:rows] * root_scale
+
+    value_total, out_total = total[:wide], total[wide:]
     for k in reversed(z_peers):
         pltpu.make_async_copy(zbuf.at[k], zbuf.at[k], zrecv.at[3, k]).wait()
-        total = total + zbuf[k]
-    rest = total[2 * rows :]
+        value_total = value_total + zbuf[k]
+        pltpu.make_async_copy(obuf.at[k], obuf.at[k], zrecv.at[4, k]).wait()
+        out_total = out_total + obuf[k].astype(f32)[:rows]
+    rest = value_total[rows : rows + fold]
     rest = jnp.concatenate([rest[:, 32 * g : 32 * (g + 1)] for g in range(4)], axis=0)
-    value_out[...] = jnp.concatenate([total[:rows], rest[:, :16]], axis=1)
-    out_out[...] = jnp.concatenate([total[rows : 2 * rows], rest[:, 16:]], axis=1)
+    value_out[...] = jnp.concatenate([value_total[:rows], rest[:, :16]], axis=1)
+    out_out[...] = jnp.concatenate([out_total, rest[:, 16:]], axis=1)
     for copy in sent:
         copy.wait_send()
 
@@ -382,8 +402,8 @@
     chunks = group // CHUNK
     width = w_key.shape[0]
     rows = D // nz // QUAD
-    slab = 2 * rows + rows // 4
-    wire = -(-slab // 16) * 16
+    part = -(-(rows + rows // 4) // 16) * 16
+    slab = part + rows
     slots = chunks * SLOTS
     dma = pltpu.SemaphoreType.DMA
     return pl.pallas_call(
@@ -421,20 +441,23 @@
             pltpu.VMEM((nn, ROWS, D), f32),
             pltpu.VMEM((nz, 2, 2, slab, 128), f32),
             pltpu.VMEM((nz, 2, slab, 128), f32),
-            pltpu.VMEM((nz, wire, 128), bf16),
-            pltpu.VMEM((nz, wire, 128), bf16),
-            pltpu.VMEM((nz, slab, 128), f32),
-            pltpu.VMEM((nz, slab, 128), f32),
+            pltpu.VMEM((nz, 2 * part, 128), bf16),
+            pltpu.VMEM((nz, 2 * part, 128), bf16),
+            pltpu.VMEM((nz, part, 128), f32),
+            pltpu.VMEM((nz, part, 128), f32),
+            pltpu.VMEM((nz, part, 128), bf16),
+            pltpu.VMEM((nz, part, 128), bf16),
+            pltpu.VMEM((D, nz * 128), bf16),
             pltpu.VMEM((chunks, 2 * SLOTS, width), bf16),
             pltpu.VMEM((2, D), f32),
             pltpu.VMEM((QUAD, 2, D), f32),
-            pltpu.VMEM((2, D), f32),
-            pltpu.VMEM((nz, 2, D), f32),
+            pltpu.VMEM((nz, 2, 128), f32),
+            pltpu.VMEM((nz, 2, 128), f32),
             dma((chunks + 3,)),
             dma((4, nn)),
             dma((4, nn)),
-            dma((4, nz)),
-            dma((4, nz)),
+            dma((5, nz)),
+            dma((5, nz)),
             dma((3, QUAD)),
             dma((3, QUAD)),
             dma((nz,)),

time: 64.8 us -> 63.8 us (0.985)
  Pallas kernels: 64 us -> 62.9 us
    pallas_call x1, Pallas kernels: 62.5 us -> 61.4 us  [call(): pl.pallas_call(functools.partial(kernel, nz, nn), out_shape=(jax.ShapeDty...]
where the time goes in v5:
time: 63.8 us; the launch traced here: 63.6 us
  Pallas kernels  62.9 us (99%)
  between operations  0.64 us (1%)
    pallas_call x1, Pallas kernels, call(): pl.pallas_call(functools.partial(kernel, nz, nn), out_shape=(jax.ShapeDty...  61.4 us
    pallas_call x1, Pallas kernels, finish(): pl.pallas_call(finish_kernel, out_shape=tuple((jax.ShapeDtypeStruct(a.sha...  1.5 us

profile of v5, /device:TPU:1, one launch (start us, length us, event | category | flops | bytes accessed | tf_op | source)
XLA Modules:
  0.0 63.6 jit_solution(18441986319245728019)
XLA Ops:
  0.6 61.4 %shard_map.101 = (f32[1,4]{1,0:T(1,128)}, f32[4,1152]{1,0:T(4,128)}, f32[36,144]{1,0:T(8,128)}, f32[36,144]{1,0:T(8,128)}, f32[36,144]{1,0:T(8,128)}) custom-call(bf16[8192,1152]{1,0:T(8,128)(2,1)} %bitcast.5, bf16[144,1152]{1,0:T(8,128)(2,1)} %bitcast.6, bf16[144,1152]{1,0:T(8,128)(2,1)} %bitcast.7, bf16[144,1152]{1,0:T(8,128)(2,1)} %w_out.1, ...), custom_call_target="tpu_custom_call" | custom-call | tf_op jit(solution)/shard_map/pallas_call | solution.py:409
  62.1 1.5 %shard_map.102 = (f32[1,4]{1,0:T(1,128)}, f32[4,1152]{1,0:T(4,128)}, f32[36,144]{1,0:T(8,128)}, f32[36,144]{1,0:T(8,128)}, f32[36,144]{1,0:T(8,128)}) custom-call(f32[1,4]{1,0:T(1,128)} %get-tuple-element.15.refs_0_, f32[4,1152]{1,0:T(4,128)} %get-tuple-element.16.refs_1_, f32[36,144]{1,0:T(8,128)} %get-tuple-element.17.refs_2_, ...), custom_call_target="tpu_custom_call" | custom-call | tf_op jit(solution)/shard_map/pallas_call | solution.py:389

commit v6 on v5

--- a/solution.py
+++ b/solution.py
@@ -308,7 +308,6 @@
         return jnp.concatenate([one, two, values - one - two, jnp.zeros_like(one)], axis=0).astype(bf16)
 
     score_sum = none(2 * SLOTS, D)
-    moved = 0
     for j in range(chunks):
         weight_grad = matmul(head_rows[j], values[j])
         weight_grad = weight_grad[:SLOTS] + weight_grad[SLOTS:]
@@ -318,27 +317,21 @@
         top = score_grad.astype(bf16).astype(f32)
         pair = jnp.concatenate([top, score_grad - top], axis=0).astype(bf16)
         score_sum = score_sum + matmul(pair, held[j])
-        if j > 0:
-            while moved < nz * j // chunks:
-                total = onward(moved)
-                moved += 1
+        if j == chunks // 2:
+            arrived(z_peers, ubuf, zrecv.at[1])
+            quad_grad = usrc[z].astype(f32)
+            for k in z_peers:
+                quad_grad = quad_grad + ubuf[k].astype(f32)
+            for k in range(QUAD):
+                vsrc[k] = quad_grad[k * ROWS : (k + 1) * ROWS]
+            exchange(q_peers, at_q, q, lambda k: vsrc.at[k], vbuf, qsend.at[1], qrecv.at[1])
     per_head = score_sum[:SLOTS] + score_sum[SLOTS:]
     for h in range(2):
         ssum[h : h + 1] = jnp.sum(per_head[h * CHUNK : (h + 1) * CHUNK], axis=0, keepdims=True)
     sbuf[q] = ssum[...]
     exchange(q_peers, at_q, q, lambda k: ssum, sbuf, qsend.at[2], qrecv.at[2])
-    while moved < nz:
-        total = onward(moved)
-        moved += 1
-
-    arrived(z_peers, ubuf, zrecv.at[1])
-    quad_grad = usrc[z].astype(f32)
-    for k in z_peers:
-        quad_grad = quad_grad + ubuf[k].astype(f32)
-    for k in range(QUAD):
-        vsrc[k] = quad_grad[k * ROWS : (k + 1) * ROWS]
-    exchange(q_peers, at_q, q, lambda k: vsrc.at[k], vbuf, qsend.at[1], qrecv.at[1])
-
+    for i in range(nz // 2):
+        onward(i)
     arrived(q_peers, sbuf, qrecv.at[2])
     scores_all = sbuf[0] + sbuf[1] + sbuf[2] + sbuf[3]
     picked = matmul(three_parts(scores_all), pick[...])
@@ -346,6 +339,8 @@
         mine = picked[:, k * 128 : (k + 1) * 128]
         szsum[k] = mine[0:2] + mine[2:4] + mine[4:6]
     exchange(z_peers, at_z, z, lambda k: szsum.at[k], szbuf, zsend.at[2], zrecv.at[2])
+    for i in range(nz // 2, nz):
+        total = onward(i)
     arrived(q_peers, vbuf, qrecv.at[1])
     unit_grad = vsrc[q]
     for k in q_peers:

time: 63.8 us -> 65.5 us (1.027)
  Pallas kernels: 62.9 us -> 64.7 us
    pallas_call x1, Pallas kernels: 61.4 us -> 63.2 us  [call(): pl.pallas_call(functools.partial(kernel, nz, nn), out_shape=(jax.ShapeDty...]
where the time goes in v6:
time: 65.5 us; the launch traced here: 65.3 us
  Pallas kernels  64.7 us (99%)
    pallas_call x1, Pallas kernels, call(): pl.pallas_call(functools.partial(kernel, nz, nn), out_shape=(jax.ShapeDty...  63.2 us
    pallas_call x1, Pallas kernels, finish(): pl.pallas_call(finish_kernel, out_shape=tuple((jax.ShapeDtypeStruct(a.sha...  1.5 us

profile of v6, /device:TPU:1, one launch (start us, length us, event | category | flops | bytes accessed | tf_op | source)
XLA Modules:
  0.0 65.3 jit_solution(843291723435164965)
XLA Ops:
  0.6 63.2 %shard_map.101 = (f32[1,4]{1,0:T(1,128)}, f32[4,1152]{1,0:T(4,128)}, f32[36,144]{1,0:T(8,128)}, f32[36,144]{1,0:T(8,128)}, f32[36,144]{1,0:T(8,128)}) custom-call(bf16[8192,1152]{1,0:T(8,128)(2,1)} %bitcast.5, bf16[144,1152]{1,0:T(8,128)(2,1)} %bitcast.6, bf16[144,1152]{1,0:T(8,128)(2,1)} %bitcast.7, bf16[144,1152]{1,0:T(8,128)(2,1)} %w_out.1, ...), custom_call_target="tpu_custom_call" | custom-call | tf_op jit(solution)/shard_map/pallas_call | solution.py:404
  63.8 1.5 %shard_map.102 = (f32[1,4]{1,0:T(1,128)}, f32[4,1152]{1,0:T(4,128)}, f32[36,144]{1,0:T(8,128)}, f32[36,144]{1,0:T(8,128)}, f32[36,144]{1,0:T(8,128)}) custom-call(f32[1,4]{1,0:T(1,128)} %get-tuple-element.15.refs_0_, f32[4,1152]{1,0:T(4,128)} %get-tuple-element.16.refs_1_, f32[36,144]{1,0:T(8,128)} %get-tuple-element.17.refs_2_, ...), custom_call_target="tpu_custom_call" | custom-call | tf_op jit(solution)/shard_map/pallas_call | solution.py:384

commit v7 on v5

--- a/solution.py
+++ b/solution.py
@@ -78,8 +78,12 @@
     chunks = group // CHUNK
     width = w_key.shape[0]
     root_scale = 1.0 / math.sqrt(HEAD_DIM)
-    narrow_peers = [lax.rem(n + d, nn) for d in range(1, nn)]
-    z_peers = [lax.rem(z + d, nz) for d in range(1, nz)]
+    ring = nn // 2
+    steps = [(a, d) for a in range(2) for d in range(ring) if a + d > 0]
+    steps.sort(key=lambda step: -(step[0] + min(step[1], ring - step[1])))
+    narrow_peers = [lax.rem(n // ring + a, 2) * ring + lax.rem(n + d, ring) for a, d in steps]
+    z_steps = sorted(range(1, nz), key=lambda d: -min(d, nz - d))
+    z_peers = [lax.rem(z + d, nz) for d in z_steps]
     q_peers = [lax.rem(q + d, QUAD) for d in range(1, QUAD)]
     at_n = lambda k: {"wide": w, "narrow": k}
     at_z = lambda k: {"wide": k * QUAD + q, "narrow": n}
@@ -318,10 +322,9 @@
         top = score_grad.astype(bf16).astype(f32)
         pair = jnp.concatenate([top, score_grad - top], axis=0).astype(bf16)
         score_sum = score_sum + matmul(pair, held[j])
-        if j > 0:
-            while moved < nz * j // chunks:
-                total = onward(moved)
-                moved += 1
+        while moved < j - 2:
+            onward(moved)
+            moved += 1
     per_head = score_sum[:SLOTS] + score_sum[SLOTS:]
     for h in range(2):
         ssum[h : h + 1] = jnp.sum(per_head[h * CHUNK : (h + 1) * CHUNK], axis=0, keepdims=True)
@@ -330,7 +333,13 @@
     while moved < nz:
         total = onward(moved)
         moved += 1
-
+    arrived(q_peers, sbuf, qrecv.at[2])
+    scores_all = sbuf[0] + sbuf[1] + sbuf[2] + sbuf[3]
+    picked = matmul(three_parts(scores_all), pick[...])
+    for k in range(nz):
+        mine = picked[:, k * 128 : (k + 1) * 128]
+        szsum[k] = mine[0:2] + mine[2:4] + mine[4:6]
+    exchange(z_peers, at_z, z, lambda k: szsum.at[k], szbuf, zsend.at[2], zrecv.at[2])
     arrived(z_peers, ubuf, zrecv.at[1])
     quad_grad = usrc[z].astype(f32)
     for k in z_peers:
@@ -339,13 +348,6 @@
         vsrc[k] = quad_grad[k * ROWS : (k + 1) * ROWS]
     exchange(q_peers, at_q, q, lambda k: vsrc.at[k], vbuf, qsend.at[1], qrecv.at[1])
 
-    arrived(q_peers, sbuf, qrecv.at[2])
-    scores_all = sbuf[0] + sbuf[1] + sbuf[2] + sbuf[3]
-    picked = matmul(three_parts(scores_all), pick[...])
-    for k in range(nz):
-        mine = picked[:, k * 128 : (k + 1) * 128]
-        szsum[k] = mine[0:2] + mine[2:4] + mine[4:6]
-    exchange(z_peers, at_z, z, lambda k: szsum.at[k], szbuf, zsend.at[2], zrecv.at[2])
     arrived(q_peers, vbuf, qrecv.at[1])
     unit_grad = vsrc[q]
     for k in q_peers:

time: 63.8 us -> 63 us (0.987)
  Pallas kernels: 62.9 us -> 62.2 us
    pallas_call x1, Pallas kernels: 61.4 us -> 60.7 us  [call(): pl.pallas_call(functools.partial(kernel, nz, nn), out_shape=(jax.ShapeDty...]
where the time goes in v7:
time: 63 us; the launch traced here: 62.8 us
  Pallas kernels  62.2 us (99%)
  between operations  0.64 us (1%)
    pallas_call x1, Pallas kernels, call(): pl.pallas_call(functools.partial(kernel, nz, nn), out_shape=(jax.ShapeDty...  60.7 us
    pallas_call x1, Pallas kernels, finish(): pl.pallas_call(finish_kernel, out_shape=tuple((jax.ShapeDtypeStruct(a.sha...  1.5 us

profile of v7, /device:TPU:1, one launch (start us, length us, event | category | flops | bytes accessed | tf_op | source)
XLA Modules:
  0.0 62.8 jit_solution(16910265521496439585)
XLA Ops:
  0.6 60.7 %shard_map.101 = (f32[1,4]{1,0:T(1,128)}, f32[4,1152]{1,0:T(4,128)}, f32[36,144]{1,0:T(8,128)}, f32[36,144]{1,0:T(8,128)}, f32[36,144]{1,0:T(8,128)}) custom-call(bf16[8192,1152]{1,0:T(8,128)(2,1)} %bitcast.5, bf16[144,1152]{1,0:T(8,128)(2,1)} %bitcast.6, bf16[144,1152]{1,0:T(8,128)(2,1)} %bitcast.7, bf16[144,1152]{1,0:T(8,128)(2,1)} %w_out.1, ...), custom_call_target="tpu_custom_call" | custom-call | tf_op jit(solution)/shard_map/pallas_call | solution.py:411
  61.3 1.5 %shard_map.102 = (f32[1,4]{1,0:T(1,128)}, f32[4,1152]{1,0:T(4,128)}, f32[36,144]{1,0:T(8,128)}, f32[36,144]{1,0:T(8,128)}, f32[36,144]{1,0:T(8,128)}) custom-call(f32[1,4]{1,0:T(1,128)} %get-tuple-element.15.refs_0_, f32[4,1152]{1,0:T(4,128)} %get-tuple-element.16.refs_1_, f32[36,144]{1,0:T(8,128)} %get-tuple-element.17.refs_2_, ...), custom_call_target="tpu_custom_call" | custom-call | tf_op jit(solution)/shard_map/pallas_call | solution.py:391

commit v8 on v7

--- a/solution.py
+++ b/solution.py
@@ -296,15 +296,11 @@
             sent.append(remote(osrc.at[k], obuf.at[z], zsend.at[4, k], zrecv.at[4, z], at_z(k)))
         return total
 
-    for i in range(nz):
-        block_out(order[i])
-        if i > 1:
-            forward(order[i - 2])
+    for k in order:
+        block_out(k)
     for j in range(chunks):
         pair = [high[j * SLOTS : (j + 1) * SLOTS], low[j * SLOTS : (j + 1) * SLOTS]]
         head_rows[j] = jnp.concatenate(pair, axis=0).astype(bf16)
-    forward(order[nz - 2])
-    forward(order[nz - 1])
 
     def three_parts(values):
         one = values.astype(bf16).astype(f32)
@@ -322,17 +318,20 @@
         top = score_grad.astype(bf16).astype(f32)
         pair = jnp.concatenate([top, score_grad - top], axis=0).astype(bf16)
         score_sum = score_sum + matmul(pair, held[j])
-        while moved < j - 2:
-            onward(moved)
-            moved += 1
+        upto = min(nz, 2 * (j - 1)) if j > 1 else 0
+        for k in order[moved:upto]:
+            forward(k)
+        moved = upto
     per_head = score_sum[:SLOTS] + score_sum[SLOTS:]
     for h in range(2):
         ssum[h : h + 1] = jnp.sum(per_head[h * CHUNK : (h + 1) * CHUNK], axis=0, keepdims=True)
     sbuf[q] = ssum[...]
     exchange(q_peers, at_q, q, lambda k: ssum, sbuf, qsend.at[2], qrecv.at[2])
-    while moved < nz:
-        total = onward(moved)
-        moved += 1
+    for k in order[moved:]:
+        forward(k)
+    early = nz // 2 + 1
+    for i in range(early):
+        total = onward(i)
     arrived(q_peers, sbuf, qrecv.at[2])
     scores_all = sbuf[0] + sbuf[1] + sbuf[2] + sbuf[3]
     picked = matmul(three_parts(scores_all), pick[...])
@@ -340,6 +339,8 @@
         mine = picked[:, k * 128 : (k + 1) * 128]
         szsum[k] = mine[0:2] + mine[2:4] + mine[4:6]
     exchange(z_peers, at_z, z, lambda k: szsum.at[k], szbuf, zsend.at[2], zrecv.at[2])
+    for i in range(early, nz):
+        total = onward(i)
     arrived(z_peers, ubuf, zrecv.at[1])
     quad_grad = usrc[z].astype(f32)
     for k in z_peers:

time: 63 us -> 60.8 us (0.965)
  Pallas kernels: 62.2 us -> 60 us
    pallas_call x1, Pallas kernels: 60.7 us -> 58.5 us  [call(): pl.pallas_call(functools.partial(kernel, nz, nn), out_shape=(jax.ShapeDty...]
where the time goes in v8:
time: 60.8 us; the launch traced here: 60.6 us
  Pallas kernels  60 us (99%)
  between operations  0.64 us (1%)
    pallas_call x1, Pallas kernels, call(): pl.pallas_call(functools.partial(kernel, nz, nn), out_shape=(jax.ShapeDty...  58.5 us
    pallas_call x1, Pallas kernels, finish(): pl.pallas_call(finish_kernel, out_shape=tuple((jax.ShapeDtypeStruct(a.sha...  1.5 us

profile of v8, /device:TPU:1, one launch (start us, length us, event | category | flops | bytes accessed | tf_op | source)
XLA Modules:
  0.0 60.6 jit_solution(12808478626830538452)
XLA Ops:
  0.6 58.5 %shard_map.101 = (f32[1,4]{1,0:T(1,128)}, f32[4,1152]{1,0:T(4,128)}, f32[36,144]{1,0:T(8,128)}, f32[36,144]{1,0:T(8,128)}, f32[36,144]{1,0:T(8,128)}) custom-call(bf16[8192,1152]{1,0:T(8,128)(2,1)} %bitcast.5, bf16[144,1152]{1,0:T(8,128)(2,1)} %bitcast.6, bf16[144,1152]{1,0:T(8,128)(2,1)} %bitcast.7, bf16[144,1152]{1,0:T(8,128)(2,1)} %w_out.1, ...), custom_call_target="tpu_custom_call" | custom-call | tf_op jit(solution)/shard_map/pallas_call | solution.py:412
  59.1 1.5 %shard_map.102 = (f32[1,4]{1,0:T(1,128)}, f32[4,1152]{1,0:T(4,128)}, f32[36,144]{1,0:T(8,128)}, f32[36,144]{1,0:T(8,128)}, f32[36,144]{1,0:T(8,128)}) custom-call(f32[1,4]{1,0:T(1,128)} %get-tuple-element.15.refs_0_, f32[4,1152]{1,0:T(4,128)} %get-tuple-element.16.refs_1_, f32[36,144]{1,0:T(8,128)} %get-tuple-element.17.refs_2_, ...), custom_call_target="tpu_custom_call" | custom-call | tf_op jit(solution)/shard_map/pallas_call | solution.py:392

commit v9 on v8

--- a/solution.py
+++ b/solution.py
@@ -146,7 +146,7 @@
     value_load.wait()
     for j in range(chunks):
         project(j)
-        if j == 1:
+        if j == 2:
             arrived(q_peers, qbuf, qrecv.at[0])
             tbuf[z] = jnp.concatenate([qbuf[k] for k in range(QUAD)], axis=0).astype(bf16)
             exchange(z_peers, at_z, z, lambda k: tbuf.at[z], tbuf, zsend.at[0], zrecv.at[0])
@@ -329,7 +329,7 @@
     exchange(q_peers, at_q, q, lambda k: ssum, sbuf, qsend.at[2], qrecv.at[2])
     for k in order[moved:]:
         forward(k)
-    early = nz // 2 + 1
+    early = nz // 2 - 1
     for i in range(early):
         total = onward(i)
     arrived(q_peers, sbuf, qrecv.at[2])

time: 60.8 us -> 60.3 us (level)
  no operation moved by 1% of the time
where the time goes in v9:
time: 60.3 us; the launch traced here: 60.1 us
  Pallas kernels  59.4 us (99%)
  between operations  0.64 us (1%)
    pallas_call x1, Pallas kernels, call(): pl.pallas_call(functools.partial(kernel, nz, nn), out_shape=(jax.ShapeDty...  57.9 us
    pallas_call x1, Pallas kernels, finish(): pl.pallas_call(finish_kernel, out_shape=tuple((jax.ShapeDtypeStruct(a.sha...  1.5 us

profile of v9, /device:TPU:1, one launch (start us, length us, event | category | flops | bytes accessed | tf_op | source)
XLA Modules:
  0.0 60.1 jit_solution(14345743808963739069)
XLA Ops:
  0.6 57.9 %shard_map.101 = (f32[1,4]{1,0:T(1,128)}, f32[4,1152]{1,0:T(4,128)}, f32[36,144]{1,0:T(8,128)}, f32[36,144]{1,0:T(8,128)}, f32[36,144]{1,0:T(8,128)}) custom-call(bf16[8192,1152]{1,0:T(8,128)(2,1)} %bitcast.5, bf16[144,1152]{1,0:T(8,128)(2,1)} %bitcast.6, bf16[144,1152]{1,0:T(8,128)(2,1)} %bitcast.7, bf16[144,1152]{1,0:T(8,128)(2,1)} %w_out.1, ...), custom_call_target="tpu_custom_call" | custom-call | tf_op jit(solution)/shard_map/pallas_call | solution.py:412
  58.6 1.5 %shard_map.102 = (f32[1,4]{1,0:T(1,128)}, f32[4,1152]{1,0:T(4,128)}, f32[36,144]{1,0:T(8,128)}, f32[36,144]{1,0:T(8,128)}, f32[36,144]{1,0:T(8,128)}) custom-call(f32[1,4]{1,0:T(1,128)} %get-tuple-element.15.refs_0_, f32[4,1152]{1,0:T(4,128)} %get-tuple-element.16.refs_1_, f32[36,144]{1,0:T(8,128)} %get-tuple-element.17.refs_2_, ...), custom_call_target="tpu_custom_call" | custom-call | tf_op jit(solution)/shard_map/pallas_call | solution.py:392
